TPU v7x, 32 devices: a whole 2x2x4 slice. The times are simulated.
32 devices in a mesh: lat: 8 (over z, x), coh: 4 (over y, core).
Axes of the slice: x: 2, y: 2, z: 4, core: 2. Of those that a mesh axis runs over, the one named last changes fastest.
Arguments:
- density: float32 [128, 2, 64, 1024], P('coh', None, 'lat'), may hold values from 0.1 to 1
- cotangent: float32 [128, 2, 64, 1024], P('coh', None, 'lat'), may hold values from -0.5 to 1.5
- land_mask: int32 [2, 64, 1024], P(None, 'lat'), may hold values 0 or 1
- east_vel: float32 [2, 64, 1024], P(None, 'lat'), may hold values from -0.4 to 0.4
- north_vel: float32 [2, 64, 1024], P(None, 'lat'), may hold values from -0.4 to 0.4
- diffusion: float32 [2, 64, 1024], P(None, 'lat'), may hold values from 0.02 to 0.2
- age_class: int32 [128], P('coh'), may hold values from 0 to 31, as said below
- mort_rate: float32 [32], replicated, may hold values from 0.05 to 0.5
- crowd_coef: float32 [32], replicated, may hold values from 1 to 4
- mass: float32 [32], replicated, may hold values from 0.5 to 2
- speed: float32 [32], replicated, may hold values from 0.25 to 1
Outputs:
- grad_density: float32 [128, 2, 64, 1024], P('coh', None, 'lat')
- grad_east_vel: float32 [2, 64, 1024], P(None, 'lat', 'coh')
- grad_north_vel: float32 [2, 64, 1024], P(None, 'lat', 'coh')
- grad_diffusion: float32 [2, 64, 1024], P(None, 'lat', 'coh')
Inputs may be any that keep to these rules, and one draw needn't show every extreme that they name: `age_class`: each age class is held by exactly 4 cohorts.
All inputs are finite; a program needn't handle non-finite values. No bound on the sum of `land_mask` on one device may be relied on, other than what follows from the above.
Results may differ from a plain program's by a relative error of at most 0.00014.
Values sent between devices are 32-bit elements; how exact they have to be, the bound alone decides.
A program may use at most 128 MiB of HBM per device.

v0:
```python
import jax
import jax.numpy as jnp
from jax import lax
from jax.sharding import PartitionSpec as P

COH = 128
STEPS = 2


def extended(value, sides, width):
    for axis, dim in sides:
        devices, length = (lax.axis_size(axis), value.shape[dim])
        up = [(i, (i + 1) % devices) for i in range(devices - 1)]
        down = [(j, i) for i, j in up]
        last = lax.slice_in_dim(value, length - width, length, axis=dim)
        first = lax.slice_in_dim(value, 0, width, axis=dim)
        before = lax.ppermute(last, axis, up)
        after = lax.ppermute(first, axis, down)
        value = jnp.concatenate([before, value, after], axis=dim)
    return value


def passed_along(value, axis, by):
    devices = lax.axis_size(axis)
    pairs = [(i, i + by) for i in range(devices) if 0 <= i + by < devices]
    return lax.ppermute(value, axis, pairs)


def lookup(age_class, mort_rate, crowd_coef, mass, speed):
    classes = jnp.arange(mort_rate.shape[0], dtype=jnp.int32)
    onehot = (age_class[:, None] == classes[None, :]).astype(jnp.float32)
    tables = jnp.stack([mort_rate, crowd_coef, mass, speed], axis=1)
    picked = jnp.dot(onehot, tables, precision=lax.Precision.HIGHEST)
    return [picked[:, column][:, None, None, None] for column in range(4)]


def local(
    density,
    cotangent,
    land_mask,
    east_vel,
    north_vel,
    diffusion,
    age_class,
    mort_rate,
    crowd_coef,
    mass,
    speed,
):
    ocean = land_mask.astype(jnp.float32)[None]
    mortal, crowding, weight, swim = lookup(age_class, mort_rate, crowd_coef, mass, speed)
    east_coef = swim * east_vel[None]
    north_coef = swim * north_vel[None]
    kappa = diffusion[None]
    state = density
    saved = []
    for section in range(STEPS):
        crowd = lax.psum(jnp.sum(weight * state, axis=0), "coh") / COH
        survival = jnp.exp(-(mortal + crowding * crowd[None]))
        survived = state * survival
        wet = ocean * survived
        padded = extended(wet, (("lat", 2),), 1)
        north_val = padded[:, :, 2:]
        south_val = padded[:, :, :-2]
        east_val = jnp.roll(wet, -1, axis=3)
        west_val = jnp.roll(wet, 1, axis=3)
        laplace = north_val + south_val + east_val + west_val - 4.0 * wet
        east_diff = 0.5 * (east_val - west_val)
        north_diff = 0.5 * (north_val - south_val)
        state = ocean * (wet + kappa * laplace - east_coef * east_diff - north_coef * north_diff)
        saved.append((survival, survived, laplace, east_diff, north_diff))
    adjoint = cotangent
    shares = None
    for section in reversed(range(STEPS)):
        survival, survived, laplace, east_diff, north_diff = saved[section]
        masked = ocean * adjoint
        grad_east = -jnp.sum(masked * swim * east_diff, axis=0)
        grad_north = -jnp.sum(masked * swim * north_diff, axis=0)
        grad_kappa = jnp.sum(masked * laplace, axis=0)
        pieces = (
            lax.psum_scatter(grad_east, "coh", scatter_dimension=2, tiled=True),
            lax.psum_scatter(grad_north, "coh", scatter_dimension=2, tiled=True),
            lax.psum_scatter(grad_kappa, "coh", scatter_dimension=2, tiled=True),
        )
        shares = pieces if shares is None else jax.tree.map(jnp.add, shares, pieces)
        to_north = (kappa - 0.5 * north_coef) * masked
        to_south = (kappa + 0.5 * north_coef) * masked
        to_east = (kappa - 0.5 * east_coef) * masked
        to_west = (kappa + 0.5 * east_coef) * masked
        edge_low = passed_along(to_north[:, :, -1:], "lat", 1)
        from_below = jnp.concatenate([edge_low, to_north[:, :, :-1]], axis=2)
        edge_high = passed_along(to_south[:, :, :1], "lat", -1)
        from_above = jnp.concatenate([to_south[:, :, 1:], edge_high], axis=2)
        grad_wet = (
            (1.0 - 4.0 * kappa) * masked
            + jnp.roll(to_east, 1, axis=3)
            + jnp.roll(to_west, -1, axis=3)
            + from_below
            + from_above
        )
        grad_surv = ocean * grad_wet
        pressure = lax.psum(jnp.sum(-crowding * grad_surv * survived, axis=0), "coh")
        adjoint = grad_surv * survival + weight / COH * pressure[None]
    return (adjoint, shares[0], shares[1], shares[2])


def solution(mesh):
    in_specs = (
        P("coh", None, "lat", None),
        P("coh", None, "lat", None),
        P(None, "lat", None),
        P(None, "lat", None),
        P(None, "lat", None),
        P(None, "lat", None),
        P("coh"),
        P(),
        P(),
        P(),
        P(),
    )
    out_specs = (
        P("coh", None, "lat", None),
        P(None, "lat", "coh"),
        P(None, "lat", "coh"),
        P(None, "lat", "coh"),
    )
    return jax.shard_map(local, mesh=mesh, in_specs=in_specs, out_specs=out_specs, check_vma=False)
```

profile of v0, /device:TPU:0, one launch (start us, length us, event | category | flops | bytes accessed | tf_op | source)
XLA Modules:
  0.0 277.6 jit_solution(6583846151165648333)
XLA Ops:
  7.2 0.0 all-reduce.5.cloned.1.call-start
  7.2 0.9 fusion.27
  8.2 3.5 %multiply_reduce_fusion.9 = f32[2,8,1024]{2,1,0:T(8,128)} fusion(f32[32,2,8,1024]{3,2,1,0:T(8,128)} %param.11, f32[32]{0:T(128)S(1)} %get-tuple-element.51), kind=kLoop, calls=%fused_computation.56 | loop fusion | flops 1032192 | bytes 2162816 | tf_op jit(solution)/shard_map/reduce_sum | solution.py:58
  11.6 0.0 all-reduce.5.cloned.1.call-update
  11.6 0.0 all-reduce.7.cloned.1.call-start
  11.7 0.6 multiply_subtract_fusion.1
  12.4 33.2 %all-reduce.5.cloned.1.call-done = f32[2,8,1024]{2,1,0:T(8,128)} async-done(((f32[2,8,1024]{2,1,0:T(8,128)}), f32[2,8,1024]{2,1,0:T(8,128)}) %all-reduce.5.cloned.1.call-update) | async-done | bytes 65552 | tf_op jit(solution)/shard_map/psum | solution.py:58
  45.5 0.8 broadcast_multiply_fusion.1
  46.4 3.0 %fusion.26 = f32[32,2,8,1024]{3,0,2,1:T(8,128)S(1)} fusion(f32[32,2,8,1024]{3,2,1,0:T(8,128)} %param.11, f32[2,8,1024]{2,1,0:T(8,128)S(1)} %broadcast_multiply_fusion.1, f32[32]{0:T(128)S(1)} %get-tuple-element.52, f32[32]{0:T(128)S(1)} %get-tuple-element.53, f32[2,8,1024]{2,1,0:T(8,128)S(1)} %convert_element_type.4), kind=kLoop, calls=%fused_computation.58 | loop fusion | flops 2621440 | bytes 4325632 | tf_op jit(solution)/shard_map/mul | solution.py:61
  49.4 1.3 collective-permute-start.2
  50.7 4.7 %collective-permute-start.3 = (f32[32,2,1,1024]{3,0,2,1:T(8,128)S(1)}, f32[32,2,1,1024]{3,0,2,1:T(8,128)S(1)}, u32[]{:S(2)}, u32[]{:S(2)}) collective-permute-start(f32[32,2,1,1024]{3,0,2,1:T(8,128)S(1)} %get-tuple-element.41), channel_id=1, source_target_pairs={{0,4},{4,8},{8,12},{12,16},{16,20},{20,24},{24,28},{1,5},{5,9},{9,... | collective-permute-start | bytes 786440 | tf_op jit(solution)/shard_map/ppermute | solution.py:17
  55.4 0.7 fusion.45
  56.2 0.1 fusion.46
  56.4 1.7 collective-permute-done.2
  58.1 5.8 %collective-permute-done.3 = f32[32,2,1,1024]{3,0,2,1:T(8,128)S(1)} collective-permute-done((f32[32,2,1,1024]{3,0,2,1:T(8,128)S(1)}, f32[32,2,1,1024]{3,0,2,1:T(8,128)S(1)}, u32[]{:S(2)}, u32[]{:S(2)}) %collective-permute-start.3) | collective-permute-done | bytes 262176 | tf_op jit(solution)/shard_map/ppermute | solution.py:17
  63.8 6.6 %fusion.9 = (f32[32,2,8,1024]{3,0,2,1:T(8,128)}, f32[32,2,8,1024]{3,0,2,1:T(8,128)}, f32[32,2,8,1024]{3,0,2,1:T(8,128)}, f32[32,2,8,1024]{3,0,2,1:T(8,128)}, f32...) fusion(f32[2,8,1024]{2,1,0:T(8,128)S(1)} %copy-done.16, f32[32]{0:T(128)S(1)} %get-tuple-element.50, ...), kind=kLoop, calls=%fused_computation.13 | loop fusion | flops 18333696 | bytes 19726592 | tf_op jit(solution)/shard_map/mul | solution.py:88
  70.4 0.0 all-reduce.7.cloned.1.call-update
  70.5 0.0 all-reduce.9.cloned.1.call-start
  70.5 1.7 slice.159
  72.2 1.7 slice.156
  73.9 5.1 %collective-permute-start = (f32[32,2,1,1024]{3,0,2,1:T(8,128)}, f32[32,2,1,1024]{3,0,2,1:T(8,128)}, u32[]{:S(2)}, u32[]{:S(2)}) collective-permute-start(f32[32,2,1,1024]{3,0,2,1:T(8,128)} %slice.156), channel_id=1, source_target_pairs={{0,4},{4,8},{8,12},{12,16},{16,20},{20,24},{24,28},{1,5},{5,9},{9,... | collective-permute-start | bytes 786440 | tf_op jit(solution)/shard_map/ppermute | solution.py:26
  79.0 1.3 collective-permute-start.1
  80.3 0.5 broadcast_multiply_fusion.2
  80.8 1.0 slice.155
  81.8 3.7 %slice.154 = f32[32,2,8,1023]{3,0,2,1:T(8,128)} slice(f32[32,2,8,1024]{3,0,2,1:T(8,128)} %get-tuple-element.22), slice={[0:32], [0:2], [0:8], [1:1024]} | slice | bytes 4190208 | tf_op jit(solution)/shard_map/jit(_roll_static)/slice | solution.py:97
  85.5 1.4 slice.158
  86.9 0.8 copy-done.7
  87.8 1.5 slice.157
  89.2 1.8 slice.152
  91.0 11.1 %all-reduce.7.cloned.1.call-done = f32[2,8,1024]{2,1,0:T(8,128)} async-done(((f32[2,8,1024]{2,1,0:T(8,128)}), f32[2,8,1024]{2,1,0:T(8,128)}) %all-reduce.7.cloned.1.call-update) | async-done | bytes 65552 | tf_op jit(solution)/shard_map/psum | solution.py:58
  102.1 0.8 broadcast_multiply_fusion
  102.9 7.8 %multiply_reduce_fusion.7 = (f32[2,8,1024]{2,1,0:T(8,128)}, f32[32,2,8,1024]{3,0,2,1:T(8,128)}, f32[32,2,8,1024]{3,0,2,1:T(8,128)S(1)}) fusion(f32[32,2,8,1024]{3,0,2,1:T(8,128)} %get-tuple-element.47, f32[32]{0:T(128)S(1)} %get-tuple-element.49, f32[2,8,1024]{2,1,0:T(8,128)S(1)} %broadcast_multiply_fusion, f32[32]{0:T(128)S(1)} %get-tuple-element.52, ...), kind=kLoop, calls=%fused_computation.47 | loop fusion | flops 9945088 | bytes 17039744 | tf_op jit(solution)/shard_map/reduce_sum | solution.py:102
  110.7 0.9 fusion.41
  111.6 2.8 %fusion.42 = (f32[32,2,8,1023]{3,0,2,1:T(8,128)}, f32[32,2,8,1023]{3,0,2,1:T(8,128)}) fusion(f32[32,2,8,1024]{3,0,2,1:T(8,128)S(1)} %get-tuple-element.25), kind=kLoop, calls=%fused_computation.82 | loop fusion | bytes 8380416 | tf_op jit(solution)/shard_map/jit(_roll_static)/slice | solution.py:65
  114.4 0.0 all-reduce.9.cloned.1.call-update
  114.4 0.0 all-reduce.11.cloned.1.call-start
  114.5 1.9 fusion.43
  116.4 4.1 %collective-permute-start.7 = (f32[32,2,1,1024]{3,0,2,1:T(8,128)}, f32[32,2,1,1024]{3,0,2,1:T(8,128)}, u32[]{:S(2)}, u32[]{:S(2)}) collective-permute-start(f32[32,2,1,1024]{3,0,2,1:T(8,128)} %get-tuple-element.34), channel_id=1, source_target_pairs={{0,4},{4,8},{8,12},{12,16},{16,20},{20,24},{24,28},{1,5},{5,9},{9,... | collective-permute-start | bytes 786440 | tf_op jit(solution)/shard_map/ppermute | solution.py:17
  120.4 1.5 collective-permute-start.6
  121.9 23.8 %all-reduce.9.cloned.1.call-done = f32[2,8,1024]{2,1,0:T(8,128)} async-done(((f32[2,8,1024]{2,1,0:T(8,128)}), f32[2,8,1024]{2,1,0:T(8,128)}) %all-reduce.9.cloned.1.call-update) | async-done | bytes 65552 | tf_op jit(solution)/shard_map/psum | solution.py:102
  145.7 5.2 %multiply_reduce_fusion = (f32[2,8,1024]{2,1,0:T(8,128)}, f32[2,8,1024]{2,1,0:T(8,128)}, f32[2,8,1024]{2,1,0:T(8,128)}, f32[32,2,8,1024]{3,0,2,1:T(8,128)S(1)}) fusion(f32[32,2,8,1024]{3,0,2,1:T(8,128)S(1)} %fusion.26, f32[32,2,8,1023]{3,0,2,1:T(8,128)} %copy-done.4, f32[32,2,8,1]{3,0,2,1:T(8,128)S(1)} %get-tuple-element.45, ...), kind=kLoop, calls=%fused_computation.38 | loop fusion | flops 14106624 | bytes 11403776 | tf_op jit(solution)/shard_map/reduce_sum | solution.py:79
  150.9 1.5 fusion.8
  152.5 0.6 slice.168
  153.1 0.2 slice.172
  153.4 0.2 slice.171
  153.6 0.1 slice.166
  153.8 3.7 %collective-permute-start.4 = (f32[32,2,1,1024]{3,0,2,1:T(8,128)S(1)}, f32[32,2,1,1024]{3,0,2,1:T(8,128)S(1)}, u32[]{:S(2)}, u32[]{:S(2)}) collective-permute-start(f32[32,2,1,1024]{3,0,2,1:T(8,128)S(1)} %slice.170), channel_id=1, source_target_pairs={{0,4},{4,8},{8,12},{12,16},{16,20},{20,24},{24,28},{1,5},{5,9},{9,... | collective-permute-start | bytes 786440 | tf_op jit(solution)/shard_map/ppermute | solution.py:26
  157.4 1.3 collective-permute-start.5
  158.8 4.0 %multiply_reduce_fusion.1 = (f32[2,8,1024]{2,1,0:T(8,128)S(1)}, f32[2,8,1024]{2,1,0:T(8,128)S(1)}, f32[2,8,1024]{2,1,0:T(8,128)S(1)}) fusion(f32[32,2,8,1024]{3,0,2,1:T(8,128)S(1)} %copy-done.1, f32[32,2,8,1023]{3,0,2,1:T(8,128)S(1)} %copy-done.10, f32[32,2,8,1]{3,0,2,1:T(8,128)S(1)} %copy-done.11, f32[32,2,8,1]{3,0,2,1:T(8,128)S(1)} %get-tuple-element.38, ...), kind=kLoop, calls=%fused_computation.39 | loop fusion | flops 10960896 | bytes 9175168 | tf_op jit(solution)/shard_map/reduce_sum | solution.py:79
  162.9 4.7 %collective-permute-done.4 = f32[32,2,1,1024]{3,0,2,1:T(8,128)S(1)} collective-permute-done((f32[32,2,1,1024]{3,0,2,1:T(8,128)S(1)}, f32[32,2,1,1024]{3,0,2,1:T(8,128)S(1)}, u32[]{:S(2)}, u32[]{:S(2)}) %collective-permute-start.4) | collective-permute-done | bytes 262176 | tf_op jit(solution)/shard_map/ppermute | solution.py:26
  167.6 3.5 %multiply_reduce_fusion.6 = (f32[2,8,1024]{2,1,0:T(8,128)}, f32[32,2,8,1024]{3,0,2,1:T(8,128)S(1)}) fusion(f32[32,2,8,1024]{3,2,1,0:T(8,128)S(1)} %copy-done.2, f32[32]{0:T(128)S(1)} %get-tuple-element.49, f32[2,8,1024]{2,1,0:T(8,128)S(1)} %broadcast_multiply_fusion.1, f32[32]{0:T(128)S(1)} %get-tuple-element.52, f32[32]{0:T(128)S(1)} %get-tuple-element.53, ...), kind=kLoop, calls=%fused_computation.45 | loop fusion | flops 8896512 | bytes 14942592 | tf_op jit(solution)/shard_map/reduce_sum | solution.py:102
  171.1 0.0 reduce-scatter.4.cloned.1.call-start
  171.1 0.6 negate_add_fusion.1
  171.8 0.0 reduce-scatter.8.cloned.1.call-start
  171.9 0.6 add.144
  172.5 0.0 reduce-scatter.6.cloned.1.call-start
  172.6 0.6 negate_add_fusion
  173.2 0.1 reduce-scatter.6.cloned.1.call-update
  173.3 30.3 %all-reduce.11.cloned.1.call-done = f32[2,8,1024]{2,1,0:T(8,128)} async-done(((f32[2,8,1024]{2,1,0:T(8,128)}), f32[2,8,1024]{2,1,0:T(8,128)}) %all-reduce.11.cloned.1.call-update) | async-done | bytes 65552 | tf_op jit(solution)/shard_map/psum | solution.py:102
  203.6 1.4 multiply_add_fusion
  205.0 2.5 copy.18
  207.5 18.4 %reduce-scatter.4.cloned.1.call-done = f32[2,8,256]{2,1,0:T(8,128)} async-done(((f32[2,8,1024]{2,1,0:T(8,128)}), f32[2,8,256]{2,1,0:T(8,128)}) %reduce-scatter.4.cloned.1.call-update) | async-done | bytes 16400 | tf_op jit(solution)/shard_map/reduce_scatter | solution.py:81
  225.9 22.4 %reduce-scatter.8.cloned.1.call-done = f32[2,8,256]{2,1,0:T(8,128)} async-done(((f32[2,8,1024]{2,1,0:T(8,128)}), f32[2,8,256]{2,1,0:T(8,128)}) %reduce-scatter.8.cloned.1.call-update) | async-done | bytes 16400 | tf_op jit(solution)/shard_map/reduce_scatter | solution.py:83
  248.3 22.5 %reduce-scatter.6.cloned.1.call-done = f32[2,8,256]{2,1,0:T(8,128)} async-done(((f32[2,8,1024]{2,1,0:T(8,128)}), f32[2,8,256]{2,1,0:T(8,128)}) %reduce-scatter.6.cloned.1.call-update) | async-done | bytes 16400 | tf_op jit(solution)/shard_map/reduce_scatter | solution.py:82
  (63 shorter events, 0.3 us)
Async XLA Ops:
  7.2 4.5 %copy-start.12 = (f32[2,8,1024]{2,1,0:T(8,128)S(1)}, f32[2,8,1024]{2,1,0:T(8,128)}, u32[]{:S(2)}) copy-start(f32[2,8,1024]{2,1,0:T(8,128)} %param.16) | copy-start | bytes 196612
  7.2 5.2 %copy-start.23 = (s32[2,8,1024]{2,1,0:T(8,128)S(1)}, s32[2,8,1024]{2,1,0:T(8,128)}, u32[]{:S(2)}) copy-start(s32[2,8,1024]{2,1,0:T(8,128)} %param.13) | copy-start | bytes 196612
  7.2 38.4 %all-reduce.5.cloned.1.call-start = ((), (), s32[]{:S(2)}) async-start(), calls=%async_computation.3 | async-start | bytes 131072 | tf_op jit(solution)/shard_map/psum | solution.py:58
  11.6 90.4 %all-reduce.7.cloned.1.call-start = ((), (), s32[]{:S(2)}) async-start(), calls=%async_computation.4 | async-start | bytes 131072 | tf_op jit(solution)/shard_map/psum | solution.py:58
  49.4 8.7 %collective-permute-start.2 = (f32[32,2,1,1024]{3,0,2,1:T(8,128)S(1)}, f32[32,2,1,1024]{3,0,2,1:T(8,128)S(1)}, u32[]{:S(2)}, u32[]{:S(2)}) collective-permute-start(f32[32,2,1,1024]{3,0,2,1:T(8,128)S(1)} %get-tuple-element.40), channel_id=1, source_target_pairs={{4,0},{8,4},{12,8},{16,12},{20,16},{24,20},{28,24},{5,1},{9,5},{13... | collective-permute-start | bytes 786440 | tf_op jit(solution)/shard_map/ppermute | solution.py:18
  50.7 13.1 %copy-start.16 = (f32[2,8,1024]{2,1,0:T(8,128)S(1)}, f32[2,8,1024]{2,1,0:T(8,128)}, u32[]{:S(2)}) copy-start(f32[2,8,1024]{2,1,0:T(8,128)} %param.14) | copy-start | bytes 196612
  50.7 13.1 %copy-start.18 = (f32[2,8,1024]{2,1,0:T(8,128)S(1)}, f32[2,8,1024]{2,1,0:T(8,128)}, u32[]{:S(2)}) copy-start(f32[2,8,1024]{2,1,0:T(8,128)} %param.15) | copy-start | bytes 196612
  50.7 13.1 %collective-permute-start.3 = (f32[32,2,1,1024]{3,0,2,1:T(8,128)S(1)}, f32[32,2,1,1024]{3,0,2,1:T(8,128)S(1)}, u32[]{:S(2)}, u32[]{:S(2)}) collective-permute-start(f32[32,2,1,1024]{3,0,2,1:T(8,128)S(1)} %get-tuple-element.41), channel_id=1, source_target_pairs={{0,4},{4,8},{8,12},{12,16},{16,20},{20,24},{24,28},{1,5},{5,9},{9,... | collective-permute-start | bytes 786440 | tf_op jit(solution)/shard_map/ppermute | solution.py:17
  55.4 8.4 %copy-start.5 = (f32[32,2,8,1024]{3,2,1,0:T(8,128)S(1)}, f32[32,2,8,1024]{3,2,1,0:T(8,128)}, u32[]{:S(2)}) copy-start(f32[32,2,8,1024]{3,2,1,0:T(8,128)} %param.12) | copy-start | bytes 6291460
  56.2 14.2 %copy-start.3 = (f32[32,2,8,1023]{3,0,2,1:T(8,128)}, f32[32,2,8,1023]{3,0,2,1:T(8,128)S(1)}, u32[]{:S(2)}) copy-start(f32[32,2,8,1023]{3,0,2,1:T(8,128)S(1)} %get-tuple-element.42) | copy-start | bytes 6285316
  56.2 14.2 %copy-start.4 = (f32[32,2,8,1023]{3,0,2,1:T(8,128)}, f32[32,2,8,1023]{3,0,2,1:T(8,128)S(1)}, u32[]{:S(2)}) copy-start(f32[32,2,8,1023]{3,0,2,1:T(8,128)S(1)} %get-tuple-element.43) | copy-start | bytes 6285316
  70.5 75.2 %all-reduce.9.cloned.1.call-start = ((), (), s32[]{:S(2)}) async-start(), calls=%async_computation.5 | async-start | bytes 131072 | tf_op jit(solution)/shard_map/psum | solution.py:102
  73.9 29.1 %collective-permute-start = (f32[32,2,1,1024]{3,0,2,1:T(8,128)}, f32[32,2,1,1024]{3,0,2,1:T(8,128)}, u32[]{:S(2)}, u32[]{:S(2)}) collective-permute-start(f32[32,2,1,1024]{3,0,2,1:T(8,128)} %slice.156), channel_id=1, source_target_pairs={{0,4},{4,8},{8,12},{12,16},{16,20},{20,24},{24,28},{1,5},{5,9},{9,... | collective-permute-start | bytes 786440 | tf_op jit(solution)/shard_map/ppermute | solution.py:26
  79.0 24.0 %collective-permute-start.1 = (f32[32,2,1,1024]{3,0,2,1:T(8,128)}, f32[32,2,1,1024]{3,0,2,1:T(8,128)}, u32[]{:S(2)}, u32[]{:S(2)}) collective-permute-start(f32[32,2,1,1024]{3,0,2,1:T(8,128)} %slice.159), channel_id=1, source_target_pairs={{4,0},{8,4},{12,8},{16,12},{20,16},{24,20},{28,24},{5,1},{9,5},{13... | collective-permute-start | bytes 786440 | tf_op jit(solution)/shard_map/ppermute | solution.py:26
  81.8 3.7 %copy-start.8 = (f32[32,2,8,1024]{3,0,2,1:T(8,128)S(1)}, f32[32,2,8,1024]{3,0,2,1:T(8,128)}, u32[]{:S(2)}) copy-start(f32[32,2,8,1024]{3,0,2,1:T(8,128)} %get-tuple-element.30) | copy-start | bytes 6291460
  85.5 2.3 copy-start.7
  102.9 7.8 %copy-start.15 = (f32[2,8,1024]{2,1,0:T(8,128)}, f32[2,8,1024]{2,1,0:T(8,128)S(1)}, u32[]{:S(2)}) copy-start(f32[2,8,1024]{2,1,0:T(8,128)S(1)} %broadcast_multiply_fusion) | copy-start | bytes 196612
  110.7 3.7 %copy-start = (f32[32,2,8,1024]{3,0,2,1:T(8,128)}, f32[32,2,8,1024]{3,0,2,1:T(8,128)S(1)}, u32[]{:S(2)}) copy-start(f32[32,2,8,1024]{3,0,2,1:T(8,128)S(1)} %get-tuple-element.25) | copy-start | bytes 6291460
  114.4 89.2 %all-reduce.11.cloned.1.call-start = ((), (), s32[]{:S(2)}) async-start(), calls=%async_computation.6 | async-start | bytes 131072 | tf_op jit(solution)/shard_map/psum | solution.py:102
  116.4 42.4 %collective-permute-start.7 = (f32[32,2,1,1024]{3,0,2,1:T(8,128)}, f32[32,2,1,1024]{3,0,2,1:T(8,128)}, u32[]{:S(2)}, u32[]{:S(2)}) collective-permute-start(f32[32,2,1,1024]{3,0,2,1:T(8,128)} %get-tuple-element.34), channel_id=1, source_target_pairs={{0,4},{4,8},{8,12},{12,16},{16,20},{20,24},{24,28},{1,5},{5,9},{9,... | collective-permute-start | bytes 786440 | tf_op jit(solution)/shard_map/ppermute | solution.py:17
  120.4 38.3 %collective-permute-start.6 = (f32[32,2,1,1024]{3,0,2,1:T(8,128)}, f32[32,2,1,1024]{3,0,2,1:T(8,128)}, u32[]{:S(2)}, u32[]{:S(2)}) collective-permute-start(f32[32,2,1,1024]{3,0,2,1:T(8,128)} %get-tuple-element.35), channel_id=1, source_target_pairs={{4,0},{8,4},{12,8},{16,12},{20,16},{24,20},{28,24},{5,1},{9,5},{13... | collective-permute-start | bytes 786440 | tf_op jit(solution)/shard_map/ppermute | solution.py:18
  145.7 5.2 %copy-start.13 = (f32[2,8,1024]{2,1,0:T(8,128)S(1)}, f32[2,8,1024]{2,1,0:T(8,128)}, u32[]{:S(2)}) copy-start(f32[2,8,1024]{2,1,0:T(8,128)} %param.16) | copy-start | bytes 196612
  145.7 5.2 %copy-start.17 = (f32[2,8,1024]{2,1,0:T(8,128)S(1)}, f32[2,8,1024]{2,1,0:T(8,128)}, u32[]{:S(2)}) copy-start(f32[2,8,1024]{2,1,0:T(8,128)} %param.14) | copy-start | bytes 196612
  145.7 5.2 %copy-start.19 = (f32[2,8,1024]{2,1,0:T(8,128)S(1)}, f32[2,8,1024]{2,1,0:T(8,128)}, u32[]{:S(2)}) copy-start(f32[2,8,1024]{2,1,0:T(8,128)} %param.15) | copy-start | bytes 196612
  153.1 5.7 %copy-start.11 = (f32[32,2,8,1]{3,0,2,1:T(8,128)S(1)}, f32[32,2,8,1]{3,0,2,1:T(8,128)}, u32[]{:S(2)}) copy-start(f32[32,2,8,1]{3,0,2,1:T(8,128)} %get-tuple-element.39) | copy-start | bytes 6148
  153.1 5.6 %copy-start.9 = (f32[32,2,8,1023]{3,0,2,1:T(8,128)S(1)}, f32[32,2,8,1023]{3,0,2,1:T(8,128)}, u32[]{:S(2)}) copy-start(f32[32,2,8,1023]{3,0,2,1:T(8,128)} %get-tuple-element.36) | copy-start | bytes 6285316
  153.1 5.6 %copy-start.10 = (f32[32,2,8,1023]{3,0,2,1:T(8,128)S(1)}, f32[32,2,8,1023]{3,0,2,1:T(8,128)}, u32[]{:S(2)}) copy-start(f32[32,2,8,1023]{3,0,2,1:T(8,128)} %get-tuple-element.37) | copy-start | bytes 6285316
  153.4 5.4 %copy-start.1 = (f32[32,2,8,1024]{3,0,2,1:T(8,128)S(1)}, f32[32,2,8,1024]{3,0,2,1:T(8,128)}, u32[]{:S(2)}) copy-start(f32[32,2,8,1024]{3,0,2,1:T(8,128)} %copy-done) | copy-start | bytes 6291460
  153.4 5.4 %copy-start.6 = (f32[32,2,8,1024]{3,2,1,0:T(8,128)S(1)}, f32[32,2,8,1024]{3,2,1,0:T(8,128)}, u32[]{:S(2)}) copy-start(f32[32,2,8,1024]{3,2,1,0:T(8,128)} %param.12) | copy-start | bytes 6291460
  153.8 13.8 %collective-permute-start.4 = (f32[32,2,1,1024]{3,0,2,1:T(8,128)S(1)}, f32[32,2,1,1024]{3,0,2,1:T(8,128)S(1)}, u32[]{:S(2)}, u32[]{:S(2)}) collective-permute-start(f32[32,2,1,1024]{3,0,2,1:T(8,128)S(1)} %slice.170), channel_id=1, source_target_pairs={{0,4},{4,8},{8,12},{12,16},{16,20},{20,24},{24,28},{1,5},{5,9},{9,... | collective-permute-start | bytes 786440 | tf_op jit(solution)/shard_map/ppermute | solution.py:26
  157.4 10.1 %collective-permute-start.5 = (f32[32,2,1,1024]{3,0,2,1:T(8,128)S(1)}, f32[32,2,1,1024]{3,0,2,1:T(8,128)S(1)}, u32[]{:S(2)}, u32[]{:S(2)}) collective-permute-start(f32[32,2,1,1024]{3,0,2,1:T(8,128)S(1)} %slice.173), channel_id=1, source_target_pairs={{4,0},{8,4},{12,8},{16,12},{20,16},{24,20},{28,24},{5,1},{9,5},{13... | collective-permute-start | bytes 786440 | tf_op jit(solution)/shard_map/ppermute | solution.py:26
  158.8 8.8 %copy-start.2 = (f32[32,2,8,1024]{3,2,1,0:T(8,128)S(1)}, f32[32,2,8,1024]{3,2,1,0:T(8,128)}, u32[]{:S(2)}) copy-start(f32[32,2,8,1024]{3,2,1,0:T(8,128)} %param.11) | copy-start | bytes 6291460
  158.8 8.8 %copy-start.14 = (f32[2,8,1024]{2,1,0:T(8,128)S(1)}, f32[2,8,1024]{2,1,0:T(8,128)}, u32[]{:S(2)}) copy-start(f32[2,8,1024]{2,1,0:T(8,128)} %multiply_subtract_fusion.1) | copy-start | bytes 196612
  167.6 3.6 %copy-start.22 = (f32[2,8,1024]{2,1,0:T(8,128)S(1)}, f32[2,8,1024]{2,1,0:T(8,128)}, u32[]{:S(2)}) copy-start(f32[2,8,1024]{2,1,0:T(8,128)} %get-tuple-element.11) | copy-start | bytes 196612
  167.6 4.3 %copy-start.21 = (f32[2,8,1024]{2,1,0:T(8,128)S(1)}, f32[2,8,1024]{2,1,0:T(8,128)}, u32[]{:S(2)}) copy-start(f32[2,8,1024]{2,1,0:T(8,128)} %get-tuple-element.10) | copy-start | bytes 196612
  167.6 5.0 %copy-start.20 = (f32[2,8,1024]{2,1,0:T(8,128)S(1)}, f32[2,8,1024]{2,1,0:T(8,128)}, u32[]{:S(2)}) copy-start(f32[2,8,1024]{2,1,0:T(8,128)} %get-tuple-element.12) | copy-start | bytes 196612
  167.6 36.0 %copy-start.24 = (f32[32]{0:T(128)S(1)}, f32[32]{0:T(128)}, u32[]{:S(2)}) copy-start(f32[32]{0:T(128)} %get-tuple-element.48) | copy-start | bytes 388
  171.1 54.8 %reduce-scatter.4.cloned.1.call-start = ((), (), s32[]{:S(2)}) async-start(), calls=%async_computation.7 | async-start | bytes 81920 | tf_op jit(solution)/shard_map/reduce_scatter | solution.py:81
  171.8 76.5 %reduce-scatter.8.cloned.1.call-start = ((), (), s32[]{:S(2)}) async-start(), calls=%async_computation.9 | async-start | bytes 81920 | tf_op jit(solution)/shard_map/reduce_scatter | solution.py:83
  172.5 98.3 %reduce-scatter.6.cloned.1.call-start = ((), (), s32[]{:S(2)}) async-start(), calls=%async_computation.8 | async-start | bytes 81920 | tf_op jit(solution)/shard_map/reduce_scatter | solution.py:82
Sparse Core Ops, SparseCore 0:
  11.8 33.7 all-reduce.4
  70.6 31.4 all-reduce.6
  114.6 31.0 all-reduce.8
  171.2 32.3 all-reduce.10
  206.4 19.4 reduce-scatter.3
  228.9 19.4 reduce-scatter.7
  251.3 19.4 reduce-scatter.5
where the time goes:
time: 278 us
  waiting for transfers between devices  174 us (63%)
  other arithmetic  41.2 us (15%)
  local copies, waits for them, and re-layouts  23.9 us (9%)
  starting transfers between devices  23.1 us (8%)
  between operations  14.6 us (5%)
    psum x2, waiting for transfers between devices, local(): lax.psum(jnp.sum(-crowding * grad_surv * survived, axis=0), 'coh')  54.1 us
    psum x2, waiting for transfers between devices, local(): crowd = lax.psum(jnp.sum(weight * state, axis=0), 'coh') / COH  44.2 us
    reduce_scatter x1, waiting for transfers between devices, local(): lax.psum_scatter(grad_north, 'coh', scatter_dimension=2, tiled=True)  22.5 us
    reduce_scatter x1, waiting for transfers between devices, local(): lax.psum_scatter(grad_kappa, 'coh', scatter_dimension=2, tiled=True)  22.4 us
    reduce_scatter x1, waiting for transfers between devices, local(): lax.psum_scatter(grad_east, 'coh', scatter_dimension=2, tiled=True)  18.4 us
    ppermute x4, starting transfers between devices, passed_along(): return lax.ppermute(value, axis, pairs)  11.3 us
    reduce_sum x2, other arithmetic, local(): jnp.sum(-crowding * grad_surv * survived, axis=0)  11.2 us
    reduce_sum x2, other arithmetic, local(): grad_kappa = jnp.sum(masked * laplace, axis=0)  9.28 us
  transfers between devices with their start and end apart: 15, of which 10 were waited for; matrix products, arithmetic and copies ran while one was open for 13% of the time, Pallas kernels for 0%

commit v1 on v0

v1 whole, which is shorter than its diff:
```python
import functools

import jax
import jax.numpy as jnp
from jax import lax
from jax.experimental import pallas as pl
from jax.experimental.pallas import tpu as pltpu
from jax.sharding import PartitionSpec as P

STEPS = 2
MESH = pl.DeviceIdType.MESH
DENS, FIELDS, COT1, COT2, CROWD1, CROWD2, PRESS2, EDGE = range(8)
CENTRE, KAPPA, EAST, NORTH, OCEAN = range(5)


def rolled(value, by, axis):
    return pltpu.roll(value, by % value.shape[axis], axis)


def kernel(
    n_lat,
    n_coh,
    dens,
    cot,
    land,
    east,
    north,
    diff,
    age,
    mort,
    crowd_coef,
    mass,
    speed,
    out,
    out_east,
    out_north,
    out_kappa,
    field,
    halo_field,
    params,
    state,
    surv1,
    wet1,
    lap1,
    east1,
    north1,
    kept,
    total,
    partial,
    arrived,
    grads,
    share,
    share_in,
    dens_o,
    dens_h,
    field_o,
    field_h,
    cot1_o,
    cot1_h,
    cot2_o,
    cot2_h,
    sums_o,
    sums_h,
    edge_o,
    edge_h,
    wet_edge,
    into,
    kept_h,
    lat_send,
    lat_recv,
    coh_send,
    coh_recv,
    share_send,
    share_recv,
):
    cohorts, layers, rows, lon = dens.shape
    every = cohorts * n_coh
    lat = lax.axis_index("lat")
    coh = lax.axis_index("coh")
    has_low = lat > 0
    has_high = lat < n_lat - 1
    low = jnp.maximum(lat - 1, 0)
    high = jnp.minimum(lat + 1, n_lat - 1)
    peers = [lax.rem(coh + by, n_coh) for by in range(1, n_coh)]

    barrier = pltpu.get_barrier_semaphore()
    for peer in peers:
        pl.semaphore_signal(barrier, inc=1, device_id={"coh": peer}, device_id_type=MESH)

    @pl.when(has_low)
    def _():
        pl.semaphore_signal(barrier, inc=1, device_id={"lat": low}, device_id_type=MESH)

    @pl.when(has_high)
    def _():
        pl.semaphore_signal(barrier, inc=1, device_id={"lat": high}, device_id_type=MESH)

    def copies(kind, outgoing, incoming):
        def one(side, device):
            return pltpu.make_async_remote_copy(
                src_ref=outgoing.at[side],
                dst_ref=incoming.at[1 - side],
                send_sem=lat_send.at[kind, side],
                recv_sem=lat_recv.at[kind, 1 - side],
                device_id={"lat": device},
                device_id_type=MESH,
            )

        return one(0, low), one(1, high)

    messages = {
        DENS: copies(DENS, dens_o, dens_h),
        FIELDS: copies(FIELDS, field_o, field_h),
        COT1: copies(COT1, cot1_o, cot1_h),
        COT2: copies(COT2, cot2_o, cot2_h),
        CROWD1: copies(CROWD1, sums_o.at[0], sums_h.at[0]),
        CROWD2: copies(CROWD2, sums_o.at[1], sums_h.at[1]),
        PRESS2: copies(PRESS2, sums_o.at[2], sums_h.at[2]),
        EDGE: copies(EDGE, edge_o, edge_h),
    }

    def send(kind):
        to_low, to_high = messages[kind]

        @pl.when(has_low)
        def _():
            to_low.start()

        @pl.when(has_high)
        def _():
            to_high.start()

    def receive(kind):
        to_low, to_high = messages[kind]

        @pl.when(has_low)
        def _():
            to_high.wait_recv()

        @pl.when(has_high)
        def _():
            to_low.wait_recv()

    def sent(kind):
        to_low, to_high = messages[kind]

        @pl.when(has_low)
        def _():
            to_low.wait_send()

        @pl.when(has_high)
        def _():
            to_high.wait_send()

    def exchange(which):
        return [
            pltpu.make_async_remote_copy(
                src_ref=partial.at[which],
                dst_ref=arrived.at[which, by],
                send_sem=coh_send.at[which, by],
                recv_sem=coh_recv.at[which, by],
                device_id={"coh": peer},
                device_id_type=MESH,
            )
            for by, peer in enumerate(peers)
        ]

    def summed(which):
        for copy in exchange(which):
            copy.wait_recv()
        for layer in range(layers):
            value = partial[which, layer]
            for by in range(n_coh - 1):
                value = value + arrived[which, by, layer]
            total[which, layer] = value * (1.0 / every)

    def pass_sums(which, kind):
        for layer in range(layers):
            value = total[which, layer]
            sums_o[which, 0, layer : layer + 1] = value[:1]
            sums_o[which, 1, layer : layer + 1] = value[rows - 1 :]
        send(kind)

    def pack(source, low_row, high_row, target):
        def body(cohort, carry):
            for layer in range(layers):
                spot = pl.ds(layer * cohorts + cohort, 1)
                target[0, spot, :] = source[cohort, layer, low_row : low_row + 1, :]
                target[1, spot, :] = source[cohort, layer, high_row : high_row + 1, :]
            return carry

        lax.fori_loop(0, cohorts, body, 0)

    pack(dens, 0, rows - 1, dens_o)
    for layer in range(layers):
        raw = (land[layer].astype(jnp.float32), east[layer], north[layer], diff[layer])
        for index, value in enumerate(raw):
            for depth in range(2):
                spot = slice(depth * layers + layer, depth * layers + layer + 1)
                field_o[0, index, spot, :] = value[depth : depth + 1]
                field_o[1, index, spot, :] = value[rows - 1 - depth : rows - depth]
    nobody = jnp.logical_not

    @pl.when(nobody(has_low))
    def _():
        for target in (dens_h, field_h, cot1_h, cot2_h, edge_h):
            target[0] = jnp.zeros(target.shape[1:], jnp.float32)
        for which in range(3):
            sums_h[which, 0] = jnp.zeros(sums_h.shape[2:], jnp.float32)

    @pl.when(nobody(has_high))
    def _():
        for target in (dens_h, field_h, cot1_h, cot2_h, edge_h):
            target[1] = jnp.zeros(target.shape[1:], jnp.float32)
        for which in range(3):
            sums_h[which, 1] = jnp.zeros(sums_h.shape[2:], jnp.float32)

    pl.semaphore_wait(
        barrier, n_coh - 1 + has_low.astype(jnp.int32) + has_high.astype(jnp.int32)
    )
    send(DENS)
    send(FIELDS)

    def weigh(cohort, sums):
        weight = mass[age[cohort]]
        return tuple(sums[layer] + weight * dens[cohort, layer] for layer in range(layers))

    zero = jnp.zeros((rows, lon), jnp.float32)
    sums = lax.fori_loop(0, cohorts, weigh, (zero,) * layers)
    for layer in range(layers):
        partial[0, layer] = sums[layer]
    for copy in exchange(0):
        copy.start()

    for layer in range(layers):
        ocean = land[layer].astype(jnp.float32)
        kappa = diff[layer]
        field[CENTRE, layer] = ocean * (1.0 - 4.0 * kappa)
        field[KAPPA, layer] = ocean * kappa
        field[EAST, layer] = ocean * (0.5 * east[layer])
        field[NORTH, layer] = ocean * (0.5 * north[layer])
        field[OCEAN, layer] = ocean
    for cohort in range(cohorts):
        one = age[cohort]
        for index, table in enumerate((mort, crowd_coef, mass, speed)):
            params[index, cohort : cohort + 1, :] = jnp.full((1, 128), table[one], jnp.float32)
    pack(cot, 0, rows - 1, cot1_o)
    pack(cot, 1, rows - 2, cot2_o)
    grads[...] = jnp.zeros(grads.shape, jnp.float32)

    summed(0)
    pass_sums(0, CROWD1)
    send(COT1)

    def wide(index, first):
        value = params[index, pl.ds(first, 8), :]
        return jnp.concatenate([value] * (lon // 128), axis=1)

    def spread(row):
        return jnp.broadcast_to(row, (8, lon))

    def over_groups(body):
        def one(group, carry):
            first = pl.multiple_of(group * 8, 8)
            for layer in range(layers):
                spot = pl.ds(pl.multiple_of(layer * cohorts + first, 8), 8)
                body(first, layer, spot)
            return carry

        lax.fori_loop(0, cohorts // 8, one, 0)

    def halo_row(side, index, depth, layer):
        spot = depth * layers + layer
        return spread(halo_field[side, index, spot : spot + 1, :])

    receive(FIELDS)
    for side in range(2):
        ocean = field_h[side, 0]
        kappa = field_h[side, 3]
        halo_field[side, CENTRE] = ocean * (1.0 - 4.0 * kappa)
        halo_field[side, KAPPA] = ocean * kappa
        halo_field[side, EAST] = ocean * (0.5 * field_h[side, 1])
        halo_field[side, NORTH] = ocean * (0.5 * field_h[side, 2])
        halo_field[side, OCEAN] = ocean

    def survival_h(side, which, first, layer):
        crowd = spread(sums_h[which, side, layer : layer + 1, :])
        return halo_row(side, OCEAN, 0, layer) * jnp.exp(-(wide(0, first) + wide(1, first) * crowd))

    receive(CROWD1)
    receive(DENS)

    def wet_halo(first, layer, spot):
        for side in range(2):
            into[side, spot, :] = dens_h[side, spot, :] * survival_h(side, 0, first, layer)

    over_groups(wet_halo)

    row = lax.broadcasted_iota(jnp.int32, (rows, lon), 0)
    is_first = row == 0
    is_last = row == rows - 1

    def from_before(value, edge):
        return jnp.where(is_first, edge, rolled(value, 1, 0))

    def from_after(value, edge):
        return jnp.where(is_last, edge, rolled(value, -1, 0))

    def scalars(cohort):
        one = age[cohort]
        return mort[one], crowd_coef[one], mass[one], speed[one]

    def survival(layer, which, mortal, crowding):
        return field[OCEAN, layer] * jnp.exp(-(mortal + crowding * total[which, layer]))

    def forward(cohort, sums):
        mortal, crowding, weight, swim = scalars(cohort)
        added = []
        for layer in range(layers):
            spot = pl.ds(layer * cohorts + cohort, 1)
            alive = survival(layer, 0, mortal, crowding)
            wet = dens[cohort, layer] * alive
            before = from_before(wet, into[0, spot, :])
            after = from_after(wet, into[1, spot, :])
            west_val = rolled(wet, 1, 1)
            east_val = rolled(wet, -1, 1)
            around = (before + after) + (west_val + east_val)
            east_diff = east_val - west_val
            north_diff = after - before
            value = (
                field[CENTRE, layer] * wet
                + field[KAPPA, layer] * around
                - swim * (field[EAST, layer] * east_diff + field[NORTH, layer] * north_diff)
            )
            surv1[cohort, layer] = alive
            wet1[cohort, layer] = wet
            lap1[cohort, layer] = around - 4.0 * wet
            east1[cohort, layer] = east_diff
            north1[cohort, layer] = north_diff
            state[cohort, layer] = value
            added.append(sums[layer] + weight * value)
        return tuple(added)

    sums = lax.fori_loop(0, cohorts, forward, (zero,) * layers)
    for layer in range(layers):
        partial[1, layer] = sums[layer]
    for copy in exchange(1):
        copy.start()
    send(COT2)

    def flow_in(adjoint, target):
        def body(first, layer, spot):
            swim = wide(3, first)
            for side in range(2):
                shift = swim * halo_row(side, NORTH, 0, layer)
                kappa = halo_row(side, KAPPA, 0, layer)
                coef = kappa - shift if side == 0 else kappa + shift
                target[side, spot, :] = coef * adjoint(side, first, layer, spot)

        over_groups(body)

    receive(COT1)
    flow_in(lambda side, first, layer, spot: cot1_h[side, spot, :], into)
    summed(1)
    pass_sums(1, CROWD2)

    def pulled(adjoint, swum, layer, edges):
        spread_out = field[KAPPA, layer] * adjoint
        drift = field[EAST, layer] * swum
        climb = field[NORTH, layer] * swum
        return (
            field[CENTRE, layer] * adjoint
            + rolled(spread_out - drift, 1, 1)
            + rolled(spread_out + drift, -1, 1)
            + from_before(spread_out - climb, edges[0])
            + from_after(spread_out + climb, edges[1])
        )

    def back2(cohort, sums):
        mortal, crowding, weight, swim = scalars(cohort)
        added = []
        for layer in range(layers):
            spot = pl.ds(layer * cohorts + cohort, 1)
            alive = survival(layer, 1, mortal, crowding)
            wet = state[cohort, layer] * alive
            wet_edge[0, spot, :] = wet[:1]
            wet_edge[1, spot, :] = wet[rows - 1 :]
            before = from_before(wet, 0.0)
            after = from_after(wet, 0.0)
            west_val = rolled(wet, 1, 1)
            east_val = rolled(wet, -1, 1)
            adjoint = cot[cohort, layer]
            swum = swim * adjoint
            grads[0, layer] += swum * (east_val - west_val)
            grads[1, layer] += swum * (after - before)
            grads[2, layer] += adjoint * (
                (before + after) + (west_val + east_val) - 4.0 * wet
            )
            pull = pulled(adjoint, swum, layer, (into[0, spot, :], into[1, spot, :]))
            kept[cohort, layer] = pull * alive
            added.append(sums[layer] - crowding * (pull * wet))
        return tuple(added)

    sums = lax.fori_loop(0, cohorts, back2, (zero,) * layers)
    for layer in range(layers):
        partial[2, layer] = sums[layer]
    for copy in exchange(2):
        copy.start()

    edge_o[...] = jnp.zeros(edge_o.shape, jnp.float32)

    def products(first, layer, spot):
        swim = wide(3, first)
        for side in range(2):
            product = cot1_h[side, spot, :] * wet_edge[side, spot, :]
            edge_o[side, layer] += product
            edge_o[side, layers + layer] += swim * product

    over_groups(products)
    send(EDGE)

    receive(CROWD2)
    receive(COT2)

    def back2_halo(first, layer, spot):
        swim = wide(3, first)
        for side in range(2):
            sign = 1.0 if side == 0 else -1.0
            adjoint = cot1_h[side, spot, :]
            inner = 0 if side == 0 else rows - 1
            spread_out = halo_row(side, KAPPA, 0, layer) * adjoint
            drift = halo_row(side, EAST, 0, layer) * swim * adjoint
            outer_coef = halo_row(side, KAPPA, 1, layer) - sign * swim * halo_row(side, NORTH, 1, layer)
            inner_coef = spread(field[KAPPA, layer, inner : inner + 1, :]) + sign * swim * spread(
                field[NORTH, layer, inner : inner + 1, :]
            )
            pull = (
                halo_row(side, CENTRE, 0, layer) * adjoint
                + rolled(spread_out - drift, 1, 1)
                + rolled(spread_out + drift, -1, 1)
                + outer_coef * cot2_h[side, spot, :]
                + inner_coef * cot1_o[side, spot, :]
            )
            kept_h[side, spot, :] = pull * survival_h(side, 1, first, layer)

    over_groups(back2_halo)

    summed(2)
    pass_sums(2, PRESS2)
    receive(PRESS2)
    flow_in(
        lambda side, first, layer, spot: kept_h[side, spot, :]
        + wide(2, first) * spread(sums_h[2, side, layer : layer + 1, :]),
        into,
    )

    def back1(cohort, sums):
        mortal, crowding, weight, swim = scalars(cohort)
        added = []
        for layer in range(layers):
            spot = pl.ds(layer * cohorts + cohort, 1)
            adjoint = kept[cohort, layer] + weight * total[2, layer]
            swum = swim * adjoint
            grads[0, layer] += swum * east1[cohort, layer]
            grads[1, layer] += swum * north1[cohort, layer]
            grads[2, layer] += adjoint * lap1[cohort, layer]
            pull = pulled(adjoint, swum, layer, (into[0, spot, :], into[1, spot, :]))
            out[cohort, layer] = pull * surv1[cohort, layer]
            added.append(sums[layer] - crowding * (pull * wet1[cohort, layer]))
        return tuple(added)

    sums = lax.fori_loop(0, cohorts, back1, (zero,) * layers)
    for layer in range(layers):
        partial[3, layer] = sums[layer]
    for copy in exchange(3):
        copy.start()

    receive(EDGE)
    part = lon // n_coh
    for layer in range(layers):
        ocean = field[OCEAN, layer]
        sums = [jnp.sum(edge_h[side, layer], axis=0, keepdims=True) for side in range(2)]
        swims = [jnp.sum(edge_h[side, layers + layer], axis=0, keepdims=True) for side in range(2)]
        kappa = grads[2, layer] + jnp.where(is_first, sums[0], 0.0) + jnp.where(is_last, sums[1], 0.0)
        climb = grads[1, layer] + jnp.where(is_last, swims[1], 0.0) - jnp.where(is_first, swims[0], 0.0)
        values = (-0.5 * ocean * grads[0, layer], -0.5 * ocean * climb, ocean * kappa)
        for index, value in enumerate(values):
            for to in range(n_coh):
                share[to, index, layer] = value[:, to * part : (to + 1) * part]
    shares = [
        pltpu.make_async_remote_copy(
            src_ref=share.at[peer],
            dst_ref=share_in.at[by],
            send_sem=share_send.at[by],
            recv_sem=share_recv.at[by],
            device_id={"coh": peer},
            device_id_type=MESH,
        )
        for by, peer in enumerate(peers)
    ]
    for copy in shares:
        copy.start()

    summed(3)

    def finish(cohort, carry):
        weight = mass[age[cohort]]
        for layer in range(layers):
            out[cohort, layer] += weight * total[3, layer]
        return carry

    lax.fori_loop(0, cohorts, finish, 0)

    for copy in shares:
        copy.wait_recv()
    for index, target in enumerate((out_east, out_north, out_kappa)):
        value = share[coh, index]
        for by in range(n_coh - 1):
            value = value + share_in[by, index]
        target[...] = value

    for kind in messages:
        sent(kind)
    for which in range(2 * STEPS):
        for copy in exchange(which):
            copy.wait_send()
    for copy in shares:
        copy.wait_send()


def local(*args):
    density = args[0]
    cohorts, layers, rows, lon = density.shape
    n_lat, n_coh = lax.axis_size("lat"), lax.axis_size("coh")
    f32 = jnp.float32
    vmem = pl.BlockSpec(memory_space=pltpu.VMEM)
    smem = pl.BlockSpec(memory_space=pltpu.SMEM)
    share = jax.ShapeDtypeStruct((layers, rows, lon // n_coh), f32)
    whole = pltpu.VMEM(density.shape, f32)
    packed = pltpu.VMEM((2, layers * cohorts, lon), f32)
    scratch = [
        pltpu.VMEM((5, layers, rows, lon), f32),
        pltpu.VMEM((2, 5, 2 * layers, lon), f32),
        pltpu.VMEM((4, cohorts, 128), f32),
        whole,
        whole,
        whole,
        whole,
        whole,
        whole,
        whole,
        pltpu.VMEM((4, layers, rows, lon), f32),
        pltpu.VMEM((4, layers, rows, lon), f32),
        pltpu.VMEM((4, n_coh - 1, layers, rows, lon), f32),
        pltpu.VMEM((3, layers, rows, lon), f32),
        pltpu.VMEM((n_coh, 3, layers, rows, lon // n_coh), f32),
        pltpu.VMEM((n_coh - 1, 3, layers, rows, lon // n_coh), f32),
        packed,
        packed,
        pltpu.VMEM((2, 4, 2 * layers, lon), f32),
        pltpu.VMEM((2, 4, 2 * layers, lon), f32),
        packed,
        packed,
        packed,
        packed,
        pltpu.VMEM((3, 2, layers, lon), f32),
        pltpu.VMEM((3, 2, layers, lon), f32),
        pltpu.VMEM((2, 2 * layers, 8, lon), f32),
        pltpu.VMEM((2, 2 * layers, 8, lon), f32),
        packed,
        packed,
        packed,
        pltpu.SemaphoreType.DMA((8, 2)),
        pltpu.SemaphoreType.DMA((8, 2)),
        pltpu.SemaphoreType.DMA((4, n_coh - 1)),
        pltpu.SemaphoreType.DMA((4, n_coh - 1)),
        pltpu.SemaphoreType.DMA((n_coh - 1,)),
        pltpu.SemaphoreType.DMA((n_coh - 1,)),
    ]
    return pl.pallas_call(
        functools.partial(kernel, n_lat, n_coh),
        out_shape=(jax.ShapeDtypeStruct(density.shape, f32), share, share, share),
        in_specs=[vmem] * 6 + [smem] * 5,
        out_specs=(vmem,) * 4,
        scratch_shapes=scratch,
        compiler_params=pltpu.CompilerParams(
            collective_id=0, has_side_effects=True, vmem_limit_bytes=56 * 1024 * 1024
        ),
        cost_estimate=pl.CostEstimate(
            flops=150 * density.size, bytes_accessed=12 * density.size, transcendentals=2 * density.size
        ),
    )(*args)


def solution(mesh):
    fields = P(None, "lat", None)
    in_specs = (P("coh", None, "lat", None),) * 2 + (fields,) * 4 + (P("coh"),) + (P(),) * 4
    out_specs = (P("coh", None, "lat", None),) + (P(None, "lat", "coh"),) * 3
    return jax.shard_map(local, mesh=mesh, in_specs=in_specs, out_specs=out_specs, check_vma=False)
```

time: 278 us -> 68.6 us (0.25)
  the two profiles are of different devices: /device:TPU:0 before, /device:TPU:7 now
where the time goes in v1:
time: 68.6 us; the launch traced here: 68.5 us
  Pallas kernels  62.8 us (92%)
  local copies, waits for them, and re-layouts  5 us (7%)
    pallas_call x1, Pallas kernels, local(): pl.pallas_call(functools.partial(kernel, n_lat, n_coh), out_shape=(jax.Sh...  62.8 us
    unnamed x10, local copies, waits for them, and re-layouts  5 us

profile of v1, /device:TPU:7, one launch (start us, length us, event | category | flops | bytes accessed | tf_op | source)
XLA Modules:
  0.0 68.5 jit_solution(4814846184477778286)
XLA Ops:
  0.6 62.8 %shard_map.138 = (f32[32,2,8,1024]{3,2,1,0:T(8,128)}, f32[2,8,256]{2,1,0:T(8,128)}, f32[2,8,256]{2,1,0:T(8,128)}, f32[2,8,256]{2,1,0:T(8,128)}) custom-call(f32[32,2,8,1024]{3,2,1,0:T(8,128)} %dens.1, f32[32,2,8,1024]{3,2,1,0:T(8,128)} %cot.1, s32[2,8,1024]{2,1,0:T(8,128)} %land.1, f32[2,8,1024]{2,1,0:T(8,128)} %east.1, f32[2,8,1024]{2,1,0:T(8,128)} %north.1, ...), custom_call_target="tpu_custom_call" | custom-call | flops 78643200 | bytes 6291456 | tf_op jit(solution)/shard_map/pallas_call | solution.py:580
  63.5 0.0 copy-start.2
  63.5 0.0 copy-start.1
  63.5 0.0 copy-start
  63.5 3.2 %copy.19 = f32[32,2,8,1024]{3,2,1,0:T(8,128)} copy(f32[32,2,8,1024]{3,2,1,0:T(8,128)} %get-tuple-element.8) | data formatting | bytes 4194304
  66.7 0.0 copy-done.2
  66.7 0.6 copy.20
  67.3 0.0 copy-done.1
  67.3 0.6 copy.21
  67.9 0.0 copy-done
  67.9 0.6 copy.22
Async XLA Ops:
  63.5 3.2 %copy-start.2 = (f32[2,8,256]{2,1,0:T(8,128)S(1)}, f32[2,8,256]{2,1,0:T(8,128)}, u32[]{:S(2)}) copy-start(f32[2,8,256]{2,1,0:T(8,128)} %get-tuple-element.9) | copy-start | bytes 49156
  63.5 3.8 %copy-start.1 = (f32[2,8,256]{2,1,0:T(8,128)S(1)}, f32[2,8,256]{2,1,0:T(8,128)}, u32[]{:S(2)}) copy-start(f32[2,8,256]{2,1,0:T(8,128)} %get-tuple-element.10) | copy-start | bytes 49156
  63.5 4.4 %copy-start = (f32[2,8,256]{2,1,0:T(8,128)S(1)}, f32[2,8,256]{2,1,0:T(8,128)}, u32[]{:S(2)}) copy-start(f32[2,8,256]{2,1,0:T(8,128)} %get-tuple-element.11) | copy-start | bytes 49156

commit v2 on v1

--- a/solution.py
+++ b/solution.py
@@ -9,7 +9,9 @@
 
 STEPS = 2
 MESH = pl.DeviceIdType.MESH
-DENS, FIELDS, COT1, COT2, CROWD1, CROWD2, PRESS2, EDGE = range(8)
+FIELDS, COT1, COT2, PART2, CROWD2, PRESS2, EDGE = range(7)
+KAPPA_NEAR, NORTH_NEAR, EAST_NEAR, KAPPA_FAR, NORTH_FAR, KAPPA_OWN, NORTH_OWN = range(7)
+SENT = 5
 CENTRE, KAPPA, EAST, NORTH, OCEAN = range(5)
 
 
@@ -20,8 +22,8 @@
 def kernel(
     n_lat,
     n_coh,
-    dens,
-    cot,
+    dens_in,
+    cot_in,
     land,
     east,
     north,
@@ -32,9 +34,11 @@
     mass,
     speed,
     out,
-    out_east,
-    out_north,
-    out_kappa,
+    out_press,
+    out_grads,
+    dens,
+    cot,
+    last,
     field,
     halo_field,
     params,
@@ -51,8 +55,7 @@
     grads,
     share,
     share_in,
-    dens_o,
-    dens_h,
+    dens_edge,
     field_o,
     field_h,
     cot1_o,
@@ -61,11 +64,21 @@
     cot2_h,
     sums_o,
     sums_h,
+    press_o,
+    press_h,
     edge_o,
     edge_h,
+    edge_sum,
+    beyond,
+    beyond_o,
+    beyond_in,
     wet_edge,
+    wet1_edge,
+    coefs,
+    inflow,
     into,
     kept_h,
+    local_sem,
     lat_send,
     lat_recv,
     coh_send,
@@ -74,6 +87,10 @@
     share_recv,
 ):
     cohorts, layers, rows, lon = dens.shape
+    get_cot = pltpu.make_async_copy(cot_in, cot, local_sem.at[0])
+    get_dens = pltpu.make_async_copy(dens_in, dens, local_sem.at[1])
+    get_cot.start()
+    get_dens.start()
     every = cohorts * n_coh
     lat = lax.axis_index("lat")
     coh = lax.axis_index("coh")
@@ -109,13 +126,12 @@
         return one(0, low), one(1, high)
 
     messages = {
-        DENS: copies(DENS, dens_o, dens_h),
         FIELDS: copies(FIELDS, field_o, field_h),
         COT1: copies(COT1, cot1_o, cot1_h),
         COT2: copies(COT2, cot2_o, cot2_h),
-        CROWD1: copies(CROWD1, sums_o.at[0], sums_h.at[0]),
+        PART2: copies(PART2, sums_o.at[0], sums_h.at[0]),
         CROWD2: copies(CROWD2, sums_o.at[1], sums_h.at[1]),
-        PRESS2: copies(PRESS2, sums_o.at[2], sums_h.at[2]),
+        PRESS2: copies(PRESS2, press_o, press_h),
         EDGE: copies(EDGE, edge_o, edge_h),
     }
 
@@ -174,13 +190,6 @@
                 value = value + arrived[which, by, layer]
             total[which, layer] = value * (1.0 / every)
 
-    def pass_sums(which, kind):
-        for layer in range(layers):
-            value = total[which, layer]
-            sums_o[which, 0, layer : layer + 1] = value[:1]
-            sums_o[which, 1, layer : layer + 1] = value[rows - 1 :]
-        send(kind)
-
     def pack(source, low_row, high_row, target):
         def body(cohort, carry):
             for layer in range(layers):
@@ -191,7 +200,6 @@
 
         lax.fori_loop(0, cohorts, body, 0)
 
-    pack(dens, 0, rows - 1, dens_o)
     for layer in range(layers):
         raw = (land[layer].astype(jnp.float32), east[layer], north[layer], diff[layer])
         for index, value in enumerate(raw):
@@ -199,27 +207,24 @@
                 spot = slice(depth * layers + layer, depth * layers + layer + 1)
                 field_o[0, index, spot, :] = value[depth : depth + 1]
                 field_o[1, index, spot, :] = value[rows - 1 - depth : rows - depth]
-    nobody = jnp.logical_not
-
-    @pl.when(nobody(has_low))
-    def _():
-        for target in (dens_h, field_h, cot1_h, cot2_h, edge_h):
-            target[0] = jnp.zeros(target.shape[1:], jnp.float32)
-        for which in range(3):
-            sums_h[which, 0] = jnp.zeros(sums_h.shape[2:], jnp.float32)
-
-    @pl.when(nobody(has_high))
-    def _():
-        for target in (dens_h, field_h, cot1_h, cot2_h, edge_h):
-            target[1] = jnp.zeros(target.shape[1:], jnp.float32)
-        for which in range(3):
-            sums_h[which, 1] = jnp.zeros(sums_h.shape[2:], jnp.float32)
-
+
+    for side, exists in ((0, has_low), (1, has_high)):
+
+        @pl.when(jnp.logical_not(exists))
+        def _(side=side):
+            for target in (field_h, cot1_h, cot2_h, press_h, edge_h):
+                target[side] = jnp.zeros(target.shape[1:], jnp.float32)
+            for which in range(2):
+                sums_h[which, side] = jnp.zeros(sums_h.shape[2:], jnp.float32)
+
+    get_cot.wait()
+    pack(cot, 0, rows - 1, cot1_o)
     pl.semaphore_wait(
         barrier, n_coh - 1 + has_low.astype(jnp.int32) + has_high.astype(jnp.int32)
     )
-    send(DENS)
+    send(COT1)
     send(FIELDS)
+    get_dens.wait()
 
     def weigh(cohort, sums):
         weight = mass[age[cohort]]
@@ -244,13 +249,12 @@
         one = age[cohort]
         for index, table in enumerate((mort, crowd_coef, mass, speed)):
             params[index, cohort : cohort + 1, :] = jnp.full((1, 128), table[one], jnp.float32)
-    pack(cot, 0, rows - 1, cot1_o)
     pack(cot, 1, rows - 2, cot2_o)
+    send(COT2)
+    pack(dens, 0, rows - 1, dens_edge)
     grads[...] = jnp.zeros(grads.shape, jnp.float32)
-
-    summed(0)
-    pass_sums(0, CROWD1)
-    send(COT1)
+    edge_sum[...] = jnp.zeros(edge_sum.shape, jnp.float32)
+    beyond[...] = jnp.zeros(beyond.shape, jnp.float32)
 
     def wide(index, first):
         value = params[index, pl.ds(first, 8), :]
@@ -287,14 +291,34 @@
         crowd = spread(sums_h[which, side, layer : layer + 1, :])
         return halo_row(side, OCEAN, 0, layer) * jnp.exp(-(wide(0, first) + wide(1, first) * crowd))
 
-    receive(CROWD1)
-    receive(DENS)
-
-    def wet_halo(first, layer, spot):
+    def inner(side):
+        return slice(0, 1) if side == 0 else slice(rows - 1, rows)
+
+    def column(value):
+        return jnp.sum(value, axis=0, keepdims=True)
+
+    summed(0)
+
+    def outflow(first, layer, spot):
+        swim = wide(3, first)
         for side in range(2):
-            into[side, spot, :] = dens_h[side, spot, :] * survival_h(side, 0, first, layer)
-
-    over_groups(wet_halo)
+            crowd = spread(total[0, layer, inner(side), :])
+            ocean = spread(field[OCEAN, layer, inner(side), :])
+            wet = dens_edge[side, spot, :] * (ocean * jnp.exp(-(wide(0, first) + wide(1, first) * crowd)))
+            shift = swim * halo_row(side, NORTH, 0, layer)
+            kappa = halo_row(side, KAPPA, 0, layer)
+            coef = kappa - shift if side == 0 else kappa + shift
+            value = coef * wet
+            wet1_edge[side, spot, :] = wet
+            coefs[side, spot, :] = coef
+            inflow[side, spot, :] = value
+            beyond[0, side, layer] += wide(2, first) * value
+
+    over_groups(outflow)
+    for side in range(2):
+        for layer in range(layers):
+            sums_o[0, side, layer : layer + 1] = column(beyond[0, side, layer])
+    send(PART2)
 
     row = lax.broadcasted_iota(jnp.int32, (rows, lon), 0)
     is_first = row == 0
@@ -317,11 +341,10 @@
         mortal, crowding, weight, swim = scalars(cohort)
         added = []
         for layer in range(layers):
-            spot = pl.ds(layer * cohorts + cohort, 1)
             alive = survival(layer, 0, mortal, crowding)
             wet = dens[cohort, layer] * alive
-            before = from_before(wet, into[0, spot, :])
-            after = from_after(wet, into[1, spot, :])
+            before = from_before(wet, 0.0)
+            after = from_after(wet, 0.0)
             west_val = rolled(wet, 1, 1)
             east_val = rolled(wet, -1, 1)
             around = (before + after) + (west_val + east_val)
@@ -342,27 +365,27 @@
         return tuple(added)
 
     sums = lax.fori_loop(0, cohorts, forward, (zero,) * layers)
+    receive(PART2)
     for layer in range(layers):
-        partial[1, layer] = sums[layer]
+        partial[1, layer] = sums[layer] + (
+            jnp.where(is_first, sums_h[0, 0, layer : layer + 1, :], 0.0)
+            + jnp.where(is_last, sums_h[0, 1, layer : layer + 1, :], 0.0)
+        )
     for copy in exchange(1):
         copy.start()
-    send(COT2)
-
-    def flow_in(adjoint, target):
-        def body(first, layer, spot):
-            swim = wide(3, first)
-            for side in range(2):
-                shift = swim * halo_row(side, NORTH, 0, layer)
-                kappa = halo_row(side, KAPPA, 0, layer)
-                coef = kappa - shift if side == 0 else kappa + shift
-                target[side, spot, :] = coef * adjoint(side, first, layer, spot)
-
-        over_groups(body)
 
     receive(COT1)
-    flow_in(lambda side, first, layer, spot: cot1_h[side, spot, :], into)
+
+    def inflow_cot(first, layer, spot):
+        for side in range(2):
+            into[side, spot, :] = coefs[side, spot, :] * cot1_h[side, spot, :]
+
+    over_groups(inflow_cot)
     summed(1)
-    pass_sums(1, CROWD2)
+    for side in range(2):
+        for layer in range(layers):
+            sums_o[1, side, layer : layer + 1] = total[1, layer, inner(side), :]
+    send(CROWD2)
 
     def pulled(adjoint, swum, layer, edges):
         spread_out = field[KAPPA, layer] * adjoint
@@ -407,18 +430,6 @@
     for copy in exchange(2):
         copy.start()
 
-    edge_o[...] = jnp.zeros(edge_o.shape, jnp.float32)
-
-    def products(first, layer, spot):
-        swim = wide(3, first)
-        for side in range(2):
-            product = cot1_h[side, spot, :] * wet_edge[side, spot, :]
-            edge_o[side, layer] += product
-            edge_o[side, layers + layer] += swim * product
-
-    over_groups(products)
-    send(EDGE)
-
     receive(CROWD2)
     receive(COT2)
 
@@ -427,32 +438,93 @@
         for side in range(2):
             sign = 1.0 if side == 0 else -1.0
             adjoint = cot1_h[side, spot, :]
-            inner = 0 if side == 0 else rows - 1
+            behind = cot2_h[side, spot, :]
+            ours = cot1_o[side, spot, :]
+            swum = swim * adjoint
             spread_out = halo_row(side, KAPPA, 0, layer) * adjoint
-            drift = halo_row(side, EAST, 0, layer) * swim * adjoint
+            drift = halo_row(side, EAST, 0, layer) * swum
             outer_coef = halo_row(side, KAPPA, 1, layer) - sign * swim * halo_row(side, NORTH, 1, layer)
-            inner_coef = spread(field[KAPPA, layer, inner : inner + 1, :]) + sign * swim * spread(
-                field[NORTH, layer, inner : inner + 1, :]
+            inner_coef = spread(field[KAPPA, layer, inner(side), :]) + sign * swim * spread(
+                field[NORTH, layer, inner(side), :]
             )
             pull = (
                 halo_row(side, CENTRE, 0, layer) * adjoint
                 + rolled(spread_out - drift, 1, 1)
                 + rolled(spread_out + drift, -1, 1)
-                + outer_coef * cot2_h[side, spot, :]
-                + inner_coef * cot1_o[side, spot, :]
+                + outer_coef * behind
+                + inner_coef * ours
             )
-            kept_h[side, spot, :] = pull * survival_h(side, 1, first, layer)
+            alive = survival_h(side, 1, first, layer)
+            kept_h[side, spot, :] = pull * alive
+            added = inflow[side, spot, :] * alive
+            west_val = rolled(added, 1, 1)
+            east_val = rolled(added, -1, 1)
+            wet = wet_edge[side, spot, :]
+            beyond[1, side, layer] -= wide(1, first) * (pull * added)
+            edge_sum[side, KAPPA_NEAR, layer] += adjoint * (wet + (west_val + east_val) - 4.0 * added)
+            edge_sum[side, NORTH_NEAR, layer] += swum * wet
+            edge_sum[side, EAST_NEAR, layer] += swum * (east_val - west_val)
+            edge_sum[side, KAPPA_FAR, layer] += behind * added
+            edge_sum[side, NORTH_FAR, layer] += swim * (behind * added)
+            edge_sum[side, KAPPA_OWN, layer] += ours * added
+            edge_sum[side, NORTH_OWN, layer] += swim * (ours * added)
 
     over_groups(back2_halo)
+    for side in range(2):
+        for layer in range(layers):
+            spot = side * layers + layer
+            beyond_o[spot : spot + 1, :] = column(beyond[1, side, layer])
+    beyonds = [
+        pltpu.make_async_remote_copy(
+            src_ref=beyond_o,
+            dst_ref=beyond_in.at[by],
+            send_sem=coh_send.at[2 * STEPS, by],
+            recv_sem=coh_recv.at[2 * STEPS, by],
+            device_id={"coh": peer},
+            device_id_type=MESH,
+        )
+        for by, peer in enumerate(peers)
+    ]
+    for copy in beyonds:
+        copy.start()
 
     summed(2)
-    pass_sums(2, PRESS2)
+    for copy in beyonds:
+        copy.wait_recv()
+    outside = beyond_o[...]
+    for by in range(n_coh - 1):
+        outside = outside + beyond_in[by]
+    outside = outside * (1.0 / every)
+    for side in range(2):
+        for layer in range(layers):
+            press_o[side, layer : layer + 1] = total[2, layer, inner(side), :]
+        press_o[side, layers : 2 * layers] = outside[side * layers : (side + 1) * layers]
+    send(PRESS2)
     receive(PRESS2)
-    flow_in(
-        lambda side, first, layer, spot: kept_h[side, spot, :]
-        + wide(2, first) * spread(sums_h[2, side, layer : layer + 1, :]),
-        into,
-    )
+    for layer in range(layers):
+        spot = slice(layers + layer, layers + layer + 1)
+        total[2, layer] += jnp.where(is_first, press_h[0, spot, :], 0.0) + jnp.where(
+            is_last, press_h[1, spot, :], 0.0
+        )
+
+    def inflow_first(first, layer, spot):
+        swim = wide(3, first)
+        for side in range(2):
+            here = slice(side * layers + layer, side * layers + layer + 1)
+            pressure = press_h[side, layer : layer + 1, :] + outside[here]
+            adjoint = kept_h[side, spot, :] + wide(2, first) * spread(pressure)
+            into[side, spot, :] = coefs[side, spot, :] * adjoint
+            product = adjoint * wet1_edge[side, spot, :]
+            edge_sum[side, KAPPA_NEAR, layer] += product
+            edge_sum[side, NORTH_NEAR, layer] += swim * product
+
+    over_groups(inflow_first)
+    for side in range(2):
+        for index in range(SENT):
+            for layer in range(layers):
+                spot = index * layers + layer
+                edge_o[side, spot : spot + 1] = column(edge_sum[side, index, layer])
+    send(EDGE)
 
     def back1(cohort, sums):
         mortal, crowding, weight, swim = scalars(cohort)
@@ -465,7 +537,7 @@
             grads[1, layer] += swum * north1[cohort, layer]
             grads[2, layer] += adjoint * lap1[cohort, layer]
             pull = pulled(adjoint, swum, layer, (into[0, spot, :], into[1, spot, :]))
-            out[cohort, layer] = pull * surv1[cohort, layer]
+            last[cohort, layer] = pull * surv1[cohort, layer]
             added.append(sums[layer] - crowding * (pull * wet1[cohort, layer]))
         return tuple(added)
 
@@ -475,15 +547,31 @@
     for copy in exchange(3):
         copy.start()
 
+    put = pltpu.make_async_copy(last, out, local_sem.at[2])
+    put.start()
+
     receive(EDGE)
     part = lon // n_coh
     for layer in range(layers):
         ocean = field[OCEAN, layer]
-        sums = [jnp.sum(edge_h[side, layer], axis=0, keepdims=True) for side in range(2)]
-        swims = [jnp.sum(edge_h[side, layers + layer], axis=0, keepdims=True) for side in range(2)]
-        kappa = grads[2, layer] + jnp.where(is_first, sums[0], 0.0) + jnp.where(is_last, sums[1], 0.0)
-        climb = grads[1, layer] + jnp.where(is_last, swims[1], 0.0) - jnp.where(is_first, swims[0], 0.0)
-        values = (-0.5 * ocean * grads[0, layer], -0.5 * ocean * climb, ocean * kappa)
+        near = (is_first, is_last)
+        behind = (row == 1, row == rows - 2)
+        drift, climb, kappa = (grads[index, layer] for index in range(3))
+        for side in range(2):
+
+            def got(index):
+                spot = index * layers + layer
+                return edge_h[side, spot : spot + 1, :]
+
+            sign = -1.0 if side == 0 else 1.0
+            kappa_near = got(KAPPA_NEAR) + column(edge_sum[side, KAPPA_OWN, layer])
+            north_near = sign * (got(NORTH_NEAR) + column(edge_sum[side, NORTH_OWN, layer]))
+            drift = drift + jnp.where(near[side], got(EAST_NEAR), 0.0)
+            climb = climb + jnp.where(near[side], north_near, 0.0)
+            climb = climb + jnp.where(behind[side], sign * got(NORTH_FAR), 0.0)
+            kappa = kappa + jnp.where(near[side], kappa_near, 0.0)
+            kappa = kappa + jnp.where(behind[side], got(KAPPA_FAR), 0.0)
+        values = (-0.5 * ocean * drift, -0.5 * ocean * climb, ocean * kappa)
         for index, value in enumerate(values):
             for to in range(n_coh):
                 share[to, index, layer] = value[:, to * part : (to + 1) * part]
@@ -502,30 +590,37 @@
         copy.start()
 
     summed(3)
-
-    def finish(cohort, carry):
-        weight = mass[age[cohort]]
-        for layer in range(layers):
-            out[cohort, layer] += weight * total[3, layer]
-        return carry
-
-    lax.fori_loop(0, cohorts, finish, 0)
-
+    out_press[...] = total[3]
     for copy in shares:
         copy.wait_recv()
-    for index, target in enumerate((out_east, out_north, out_kappa)):
+    for index in range(3):
         value = share[coh, index]
         for by in range(n_coh - 1):
             value = value + share_in[by, index]
-        target[...] = value
-
+        out_grads[index] = value
+
+    put.wait()
     for kind in messages:
         sent(kind)
     for which in range(2 * STEPS):
         for copy in exchange(which):
             copy.wait_send()
-    for copy in shares:
+    for copy in shares + beyonds:
         copy.wait_send()
+
+
+def finish(age, mass, last, press, grads, out, out_east, out_north, out_kappa):
+    group, layers = out.shape[0], out.shape[1]
+    step = pl.program_id(0)
+    for cohort in range(group):
+        weight = mass[age[step * group + cohort]]
+        for layer in range(layers):
+            out[cohort, layer] = last[cohort, layer] + weight * press[layer]
+
+    @pl.when(step == 0)
+    def _():
+        for index, target in enumerate((out_east, out_north, out_kappa)):
+            target[...] = grads[index]
 
 
 def local(*args):
@@ -538,58 +633,91 @@
     share = jax.ShapeDtypeStruct((layers, rows, lon // n_coh), f32)
     whole = pltpu.VMEM(density.shape, f32)
     packed = pltpu.VMEM((2, layers * cohorts, lon), f32)
+    def vec(*shape):
+        return pltpu.VMEM(shape, f32)
+
+    part = lon // n_coh
+    hbm = pl.BlockSpec(memory_space=pl.ANY)
     scratch = [
-        pltpu.VMEM((5, layers, rows, lon), f32),
-        pltpu.VMEM((2, 5, 2 * layers, lon), f32),
-        pltpu.VMEM((4, cohorts, 128), f32),
-        whole,
-        whole,
-        whole,
-        whole,
-        whole,
-        whole,
-        whole,
-        pltpu.VMEM((4, layers, rows, lon), f32),
-        pltpu.VMEM((4, layers, rows, lon), f32),
-        pltpu.VMEM((4, n_coh - 1, layers, rows, lon), f32),
-        pltpu.VMEM((3, layers, rows, lon), f32),
-        pltpu.VMEM((n_coh, 3, layers, rows, lon // n_coh), f32),
-        pltpu.VMEM((n_coh - 1, 3, layers, rows, lon // n_coh), f32),
-        packed,
-        packed,
-        pltpu.VMEM((2, 4, 2 * layers, lon), f32),
-        pltpu.VMEM((2, 4, 2 * layers, lon), f32),
-        packed,
-        packed,
-        packed,
-        packed,
-        pltpu.VMEM((3, 2, layers, lon), f32),
-        pltpu.VMEM((3, 2, layers, lon), f32),
-        pltpu.VMEM((2, 2 * layers, 8, lon), f32),
-        pltpu.VMEM((2, 2 * layers, 8, lon), f32),
-        packed,
-        packed,
-        packed,
-        pltpu.SemaphoreType.DMA((8, 2)),
-        pltpu.SemaphoreType.DMA((8, 2)),
-        pltpu.SemaphoreType.DMA((4, n_coh - 1)),
-        pltpu.SemaphoreType.DMA((4, n_coh - 1)),
+        whole,
+        whole,
+        whole,
+        vec(5, layers, rows, lon),
+        vec(2, 5, 2 * layers, lon),
+        vec(4, cohorts, 128),
+        whole,
+        whole,
+        whole,
+        whole,
+        whole,
+        whole,
+        whole,
+        vec(4, layers, rows, lon),
+        vec(4, layers, rows, lon),
+        vec(4, n_coh - 1, layers, rows, lon),
+        vec(3, layers, rows, lon),
+        vec(n_coh, 3, layers, rows, part),
+        vec(n_coh - 1, 3, layers, rows, part),
+        packed,
+        vec(2, 4, 2 * layers, lon),
+        vec(2, 4, 2 * layers, lon),
+        packed,
+        packed,
+        packed,
+        packed,
+        vec(2, 2, layers, lon),
+        vec(2, 2, layers, lon),
+        vec(2, 2 * layers, lon),
+        vec(2, 2 * layers, lon),
+        vec(2, SENT * layers, lon),
+        vec(2, SENT * layers, lon),
+        vec(2, 7, layers, 8, lon),
+        vec(2, 2, layers, 8, lon),
+        vec(2 * layers, lon),
+        vec(n_coh - 1, 2 * layers, lon),
+        packed,
+        packed,
+        packed,
+        packed,
+        packed,
+        packed,
+        pltpu.SemaphoreType.DMA((3,)),
+        pltpu.SemaphoreType.DMA((7, 2)),
+        pltpu.SemaphoreType.DMA((7, 2)),
+        pltpu.SemaphoreType.DMA((5, n_coh - 1)),
+        pltpu.SemaphoreType.DMA((5, n_coh - 1)),
         pltpu.SemaphoreType.DMA((n_coh - 1,)),
         pltpu.SemaphoreType.DMA((n_coh - 1,)),
     ]
-    return pl.pallas_call(
+    size = density.size
+    last, press, grads = pl.pallas_call(
         functools.partial(kernel, n_lat, n_coh),
-        out_shape=(jax.ShapeDtypeStruct(density.shape, f32), share, share, share),
-        in_specs=[vmem] * 6 + [smem] * 5,
-        out_specs=(vmem,) * 4,
+        out_shape=(
+            jax.ShapeDtypeStruct(density.shape, f32),
+            jax.ShapeDtypeStruct((layers, rows, lon), f32),
+            jax.ShapeDtypeStruct((3, layers, rows, part), f32),
+        ),
+        in_specs=[hbm] * 2 + [vmem] * 4 + [smem] * 5,
+        out_specs=(hbm, vmem, vmem),
         scratch_shapes=scratch,
         compiler_params=pltpu.CompilerParams(
             collective_id=0, has_side_effects=True, vmem_limit_bytes=56 * 1024 * 1024
         ),
         cost_estimate=pl.CostEstimate(
-            flops=150 * density.size, bytes_accessed=12 * density.size, transcendentals=2 * density.size
+            flops=150 * size, bytes_accessed=12 * size, transcendentals=2 * size
         ),
     )(*args)
+    group = max(1, cohorts // 8)
+    block = pl.BlockSpec((group, layers, rows, lon), lambda step: (step, 0, 0, 0))
+    return pl.pallas_call(
+        finish,
+        grid=(cohorts // group,),
+        out_shape=(jax.ShapeDtypeStruct(density.shape, f32), share, share, share),
+        in_specs=[smem, smem, block, vmem, vmem],
+        out_specs=(block, vmem, vmem, vmem),
+        compiler_params=pltpu.CompilerParams(vmem_limit_bytes=56 * 1024 * 1024),
+        cost_estimate=pl.CostEstimate(flops=2 * size, bytes_accessed=8 * size, transcendentals=0),
+    )(args[6], args[9], last, press, grads)
 
 
 def solution(mesh):

time: 68.6 us -> 67.9 us (0.990)
  the two profiles are of different devices: /device:TPU:7 before, /device:TPU:0 now
where the time goes in v2:
time: 67.9 us; the launch traced here: 67 us
  Pallas kernels  66.4 us (98%)
    pallas_call x1, Pallas kernels, local(): pl.pallas_call(functools.partial(kernel, n_lat, n_coh), out_shape=(jax.Sh...  60.6 us
    pallas_call x1, Pallas kernels, local(): pl.pallas_call(finish, grid=(cohorts // group,), out_shape=(jax.ShapeDtyp...  5.78 us

profile of v2, /device:TPU:0, one launch (start us, length us, event | category | flops | bytes accessed | tf_op | source)
XLA Modules:
  0.0 67.0 jit_solution(10426375299127068214)
XLA Ops:
  0.6 60.6 %shard_map.138 = (f32[32,2,8,1024]{3,2,1,0:T(8,128)}, f32[2,8,1024]{2,1,0:T(8,128)}, f32[3,2,8,256]{3,2,1,0:T(8,128)}) custom-call(f32[32,2,8,1024]{3,2,1,0:T(8,128)} %dens_in.1, f32[32,2,8,1024]{3,2,1,0:T(8,128)} %cot_in.1, s32[2,8,1024]{2,1,0:T(8,128)} %land.1, f32[2,8,1024]{2,1,0:T(8,128)} %east.1, f32[2,8,1024]{2,1,0:T(8,128)} %north.1, ...), custom_call_target="tpu_custom_call" | custom-call | flops 78643200 | bytes 6291456 | tf_op jit(solution)/shard_map/pallas_call | solution.py:693
  61.2 5.8 %shard_map.139 = (f32[32,2,8,1024]{3,2,1,0:T(8,128)}, f32[2,8,256]{2,1,0:T(8,128)}, f32[2,8,256]{2,1,0:T(8,128)}, f32[2,8,256]{2,1,0:T(8,128)}) custom-call(s32[32]{0:T(128)} %age.3, f32[32]{0:T(128)} %mass.3, f32[32,2,8,1024]{3,2,1,0:T(8,128)} %get-tuple-element.7.last, f32[2,8,1024]{2,1,0:T(8,128)} %get-tuple-element.8.press, ...), custom_call_target="tpu_custom_call" | custom-call | flops 1048576 | bytes 4194304 | tf_op jit(solution)/shard_map/pallas_call | solution.py:712

commit v3 on v0

v3 whole, which is shorter than its diff:
```python
import functools

import jax
import jax.numpy as jnp
from jax import lax
from jax.experimental import pallas as pl
from jax.experimental.pallas import tpu as pltpu
from jax.sharding import PartitionSpec as P

STEPS = 2
MESH = pl.DeviceIdType.MESH
FIELDS, COT1, COT2, PART2, CROWD2, PRESS2, EDGE = range(7)
KAPPA_NEAR, NORTH_NEAR, EAST_NEAR, KAPPA_FAR, NORTH_FAR, KAPPA_OWN, NORTH_OWN = range(7)
SENT = 5
GROUP = 4
CHUNKS = 8
CENTRE, KAPPA, EAST, NORTH, OCEAN = range(5)


def rolled(value, by, axis):
    return pltpu.roll(value, by % value.shape[axis], axis)


def kernel(
    n_lat,
    n_coh,
    dens_in,
    cot_in,
    land,
    east,
    north,
    diff,
    age,
    mort,
    crowd_coef,
    mass,
    speed,
    out,
    out_press,
    out_grads,
    dens,
    cot,
    last,
    field,
    halo_field,
    params,
    state,
    surv1,
    wet1,
    lap1,
    east1,
    north1,
    kept,
    total,
    partial,
    arrived,
    grads,
    share,
    share_in,
    dens_edge,
    field_o,
    field_h,
    cot1_o,
    cot1_h,
    cot2_o,
    cot2_h,
    part_o,
    part_h,
    crowd_o,
    crowd_h,
    press_o,
    press_h,
    edge_o,
    edge_h,
    edge_sum,
    beyond,
    beyond_o,
    beyond_in,
    outside,
    wet_edge,
    wet1_edge,
    coefs,
    inflow,
    into,
    kept_h,
    local_sem,
    lat_send,
    lat_recv,
    coh_send,
    coh_recv,
):
    cohorts, layers, rows, lon = dens.shape
    chunk = cohorts // CHUNKS

    def fetch(source, target, which):
        return [
            pltpu.make_async_copy(
                source.at[pl.ds(at * chunk, chunk)],
                target.at[pl.ds(at * chunk, chunk)],
                local_sem.at[which, at],
            )
            for at in range(CHUNKS)
        ]

    get_dens = fetch(dens_in, dens, 0)
    get_cot = fetch(cot_in, cot, 1)
    for copy in get_dens + get_cot:
        copy.start()
    every = cohorts * n_coh
    lat = lax.axis_index("lat")
    coh = lax.axis_index("coh")
    has_low = lat > 0
    has_high = lat < n_lat - 1
    low = jnp.maximum(lat - 1, 0)
    high = jnp.minimum(lat + 1, n_lat - 1)
    peers = [lax.rem(coh + by, n_coh) for by in range(1, n_coh)]

    barrier = pltpu.get_barrier_semaphore()
    for peer in peers:
        pl.semaphore_signal(barrier, inc=1, device_id={"coh": peer}, device_id_type=MESH)

    @pl.when(has_low)
    def _():
        pl.semaphore_signal(barrier, inc=1, device_id={"lat": low}, device_id_type=MESH)

    @pl.when(has_high)
    def _():
        pl.semaphore_signal(barrier, inc=1, device_id={"lat": high}, device_id_type=MESH)

    buffers = {
        FIELDS: (field_o, field_h),
        COT1: (cot1_o, cot1_h),
        COT2: (cot2_o, cot2_h),
        PART2: (part_o, part_h),
        CROWD2: (crowd_o, crowd_h),
        PRESS2: (press_o, press_h),
        EDGE: (edge_o, edge_h),
    }

    def message(kind, layer):
        outgoing, incoming = buffers[kind]

        def one(side, device):
            return pltpu.make_async_remote_copy(
                src_ref=outgoing.at[side, layer],
                dst_ref=incoming.at[1 - side, layer],
                send_sem=lat_send.at[kind, layer, side],
                recv_sem=lat_recv.at[kind, layer, 1 - side],
                device_id={"lat": device},
                device_id_type=MESH,
            )

        return one(0, low), one(1, high)

    def send(kind, layer):
        to_low, to_high = message(kind, layer)

        @pl.when(has_low)
        def _():
            to_low.start()

        @pl.when(has_high)
        def _():
            to_high.start()

    def receive(kind, layer):
        to_low, to_high = message(kind, layer)

        @pl.when(has_low)
        def _():
            to_high.wait_recv()

        @pl.when(has_high)
        def _():
            to_low.wait_recv()

    def sent(kind, layer):
        to_low, to_high = message(kind, layer)

        @pl.when(has_low)
        def _():
            to_low.wait_send()

        @pl.when(has_high)
        def _():
            to_high.wait_send()

    def to_peers(kind, layer, source, target):
        return [
            pltpu.make_async_remote_copy(
                src_ref=source(peer),
                dst_ref=target(by),
                send_sem=coh_send.at[kind, layer, by],
                recv_sem=coh_recv.at[kind, layer, by],
                device_id={"coh": peer},
                device_id_type=MESH,
            )
            for by, peer in enumerate(peers)
        ]

    def exchange(which, layer):
        return to_peers(
            which,
            layer,
            lambda peer: partial.at[which, layer],
            lambda by: arrived.at[which, by, layer],
        )

    def exchange_beyond(layer):
        return to_peers(
            2 * STEPS, layer, lambda peer: beyond_o.at[layer], lambda by: beyond_in.at[by, layer]
        )

    def exchange_share(layer):
        return to_peers(
            2 * STEPS + 1,
            layer,
            lambda peer: share.at[peer, layer],
            lambda by: share_in.at[by, layer],
        )

    def begin(copies):
        for copy in copies:
            copy.start()

    def summed(which, layer):
        for copy in exchange(which, layer):
            copy.wait_recv()
        value = partial[which, layer]
        for by in range(n_coh - 1):
            value = value + arrived[which, by, layer]
        total[which, layer] = value * (1.0 / every)

    def pack(source, layer, low_row, high_row, target):
        def body(step, carry):
            for member in range(GROUP):
                cohort = step * GROUP + member
                spot = pl.ds(cohort, 1)
                target[0, layer, spot, :] = source[cohort, layer, low_row : low_row + 1, :]
                target[1, layer, spot, :] = source[cohort, layer, high_row : high_row + 1, :]
            return carry

        lax.fori_loop(0, cohorts // GROUP, body, 0)

    for layer in range(layers):
        raw = (land[layer].astype(jnp.float32), east[layer], north[layer], diff[layer])
        for index, value in enumerate(raw):
            for depth in range(2):
                spot = slice(2 * index + depth, 2 * index + depth + 1)
                field_o[0, layer, spot, :] = value[depth : depth + 1]
                field_o[1, layer, spot, :] = value[rows - 1 - depth : rows - depth]

    for side, exists in ((0, has_low), (1, has_high)):

        @pl.when(jnp.logical_not(exists))
        def _(side=side):
            for _, target in buffers.values():
                target[side] = jnp.zeros(target.shape[1:], jnp.float32)

    pl.semaphore_wait(
        barrier, n_coh - 1 + has_low.astype(jnp.int32) + has_high.astype(jnp.int32)
    )
    for layer in range(layers):
        send(FIELDS, layer)
    for copy in get_dens:
        copy.wait()

    zero = jnp.zeros((rows, lon), jnp.float32)

    def over_cohorts(body):
        def one(step, carry):
            return body([step * GROUP + member for member in range(GROUP)], carry)

        return lax.fori_loop(0, cohorts // GROUP, one, zero)

    def added_up(values):
        value = values[0]
        for other in values[1:]:
            value = value + other
        return value

    for layer in range(layers):

        def weigh(group, sums, layer=layer):
            return sums + added_up([mass[age[cohort]] * dens[cohort, layer] for cohort in group])

        partial[0, layer] = over_cohorts(weigh)
        begin(exchange(0, layer))

    for layer in range(layers):
        ocean = land[layer].astype(jnp.float32)
        kappa = diff[layer]
        field[CENTRE, layer] = ocean * (1.0 - 4.0 * kappa)
        field[KAPPA, layer] = ocean * kappa
        field[EAST, layer] = ocean * (0.5 * east[layer])
        field[NORTH, layer] = ocean * (0.5 * north[layer])
        field[OCEAN, layer] = ocean
    for cohort in range(cohorts):
        one = age[cohort]
        for index, table in enumerate((mort, crowd_coef, mass, speed)):
            params[index, cohort : cohort + 1, :] = jnp.full((1, 128), table[one], jnp.float32)
    for copy in get_cot:
        copy.wait()
    for layer in range(layers):
        pack(cot, layer, 0, rows - 1, cot1_o)
        send(COT1, layer)
    for layer in range(layers):
        pack(cot, layer, 1, rows - 2, cot2_o)
        send(COT2, layer)
    for layer in range(layers):
        pack(dens, layer, 0, rows - 1, dens_edge)
    grads[...] = jnp.zeros(grads.shape, jnp.float32)
    edge_sum[...] = jnp.zeros(edge_sum.shape, jnp.float32)
    beyond[...] = jnp.zeros(beyond.shape, jnp.float32)

    def wide(index, first):
        value = params[index, pl.ds(first, 8), :]
        return jnp.concatenate([value] * (lon // 128), axis=1)

    def spread(row):
        return jnp.broadcast_to(row, (8, lon))

    def over_groups(body):
        def one(group, carry):
            first = pl.multiple_of(group * 8, 8)
            body(first, pl.ds(first, 8))
            return carry

        lax.fori_loop(0, cohorts // 8, one, 0)

    def halo_row(side, index, depth, layer):
        return spread(halo_field[side, layer, 2 * index + depth : 2 * index + depth + 1, :])

    for layer in range(layers):
        receive(FIELDS, layer)
        for side in range(2):
            raw = [field_h[side, layer, 2 * index : 2 * index + 2] for index in range(4)]
            ocean, kappa = raw[0], raw[3]
            values = (
                ocean * (1.0 - 4.0 * kappa),
                ocean * kappa,
                ocean * (0.5 * raw[1]),
                ocean * (0.5 * raw[2]),
                ocean,
            )
            for index, value in enumerate(values):
                halo_field[side, layer, 2 * index : 2 * index + 2] = value

    def survival_h(side, first, layer):
        crowd = spread(crowd_h[side, layer])
        return halo_row(side, OCEAN, 0, layer) * jnp.exp(-(wide(0, first) + wide(1, first) * crowd))

    def inner(side):
        return slice(0, 1) if side == 0 else slice(rows - 1, rows)

    def column(value):
        return jnp.sum(value, axis=0, keepdims=True)

    row = lax.broadcasted_iota(jnp.int32, (rows, lon), 0)
    is_first = row == 0
    is_last = row == rows - 1

    def from_before(value, edge):
        return jnp.where(is_first, edge, rolled(value, 1, 0))

    def from_after(value, edge):
        return jnp.where(is_last, edge, rolled(value, -1, 0))

    def scalars(cohort):
        one = age[cohort]
        return mort[one], crowd_coef[one], mass[one], speed[one]

    def survival(layer, which, mortal, crowding):
        return field[OCEAN, layer] * jnp.exp(-(mortal + crowding * total[which, layer]))

    def first_step(layer):
        summed(0, layer)

        def outflow(first, spot):
            swim = wide(3, first)
            for side in range(2):
                crowd = spread(total[0, layer, inner(side), :])
                ocean = spread(field[OCEAN, layer, inner(side), :])
                alive = ocean * jnp.exp(-(wide(0, first) + wide(1, first) * crowd))
                wet = dens_edge[side, layer, spot, :] * alive
                shift = swim * halo_row(side, NORTH, 0, layer)
                kappa = halo_row(side, KAPPA, 0, layer)
                coef = kappa - shift if side == 0 else kappa + shift
                value = coef * wet
                wet1_edge[side, layer, spot, :] = wet
                coefs[side, layer, spot, :] = coef
                inflow[side, layer, spot, :] = value
                beyond[0, side, layer] += wide(2, first) * value

        over_groups(outflow)
        for side in range(2):
            part_o[side, layer] = column(beyond[0, side, layer])
        send(PART2, layer)

        def forward(group, sums):
            added = []
            for cohort in group:
                mortal, crowding, weight, swim = scalars(cohort)
                alive = survival(layer, 0, mortal, crowding)
                wet = dens[cohort, layer] * alive
                before = from_before(wet, 0.0)
                after = from_after(wet, 0.0)
                west_val = rolled(wet, 1, 1)
                east_val = rolled(wet, -1, 1)
                around = (before + after) + (west_val + east_val)
                east_diff = east_val - west_val
                north_diff = after - before
                value = (
                    field[CENTRE, layer] * wet
                    + field[KAPPA, layer] * around
                    - swim * (field[EAST, layer] * east_diff + field[NORTH, layer] * north_diff)
                )
                surv1[cohort, layer] = alive
                wet1[cohort, layer] = wet
                lap1[cohort, layer] = around - 4.0 * wet
                east1[cohort, layer] = east_diff
                north1[cohort, layer] = north_diff
                state[cohort, layer] = value
                added.append(weight * value)
            return sums + added_up(added)

        sums = over_cohorts(forward)
        receive(PART2, layer)
        partial[1, layer] = sums + (
            jnp.where(is_first, part_h[0, layer], 0.0) + jnp.where(is_last, part_h[1, layer], 0.0)
        )
        begin(exchange(1, layer))

    def pulled(adjoint, swum, layer, spot):
        spread_out = field[KAPPA, layer] * adjoint
        drift = field[EAST, layer] * swum
        climb = field[NORTH, layer] * swum
        return (
            field[CENTRE, layer] * adjoint
            + rolled(spread_out - drift, 1, 1)
            + rolled(spread_out + drift, -1, 1)
            + from_before(spread_out - climb, into[0, layer, spot, :])
            + from_after(spread_out + climb, into[1, layer, spot, :])
        )

    def second_back(layer):
        receive(COT1, layer)

        def inflow_cot(first, spot):
            for side in range(2):
                into[side, layer, spot, :] = coefs[side, layer, spot, :] * cot1_h[side, layer, spot, :]

        over_groups(inflow_cot)
        summed(1, layer)
        for side in range(2):
            crowd_o[side, layer] = total[1, layer, inner(side), :]
        send(CROWD2, layer)

        def back2(group, sums):
            added = []
            products = []
            for cohort in group:
                mortal, crowding, weight, swim = scalars(cohort)
                spot = pl.ds(cohort, 1)
                alive = survival(layer, 1, mortal, crowding)
                wet = state[cohort, layer] * alive
                wet_edge[0, layer, spot, :] = wet[:1]
                wet_edge[1, layer, spot, :] = wet[rows - 1 :]
                before = from_before(wet, 0.0)
                after = from_after(wet, 0.0)
                west_val = rolled(wet, 1, 1)
                east_val = rolled(wet, -1, 1)
                adjoint = cot[cohort, layer]
                swum = swim * adjoint
                products.append(
                    (
                        swum * (east_val - west_val),
                        swum * (after - before),
                        adjoint * ((before + after) + (west_val + east_val) - 4.0 * wet),
                    )
                )
                pull = pulled(adjoint, swum, layer, spot)
                kept[cohort, layer] = pull * alive
                added.append(crowding * (pull * wet))
            for index in range(3):
                grads[index, layer] += added_up([product[index] for product in products])
            return sums - added_up(added)

        partial[2, layer] = over_cohorts(back2)
        begin(exchange(2, layer))

    def second_beyond(layer):
        receive(CROWD2, layer)
        receive(COT2, layer)

        def back2_halo(first, spot):
            swim = wide(3, first)
            for side in range(2):
                sign = 1.0 if side == 0 else -1.0
                adjoint = cot1_h[side, layer, spot, :]
                behind = cot2_h[side, layer, spot, :]
                ours = cot1_o[side, layer, spot, :]
                swum = swim * adjoint
                spread_out = halo_row(side, KAPPA, 0, layer) * adjoint
                drift = halo_row(side, EAST, 0, layer) * swum
                outer_coef = halo_row(side, KAPPA, 1, layer) - sign * swim * halo_row(side, NORTH, 1, layer)
                inner_coef = spread(field[KAPPA, layer, inner(side), :]) + sign * swim * spread(
                    field[NORTH, layer, inner(side), :]
                )
                pull = (
                    halo_row(side, CENTRE, 0, layer) * adjoint
                    + rolled(spread_out - drift, 1, 1)
                    + rolled(spread_out + drift, -1, 1)
                    + outer_coef * behind
                    + inner_coef * ours
                )
                alive = survival_h(side, first, layer)
                kept_h[side, layer, spot, :] = pull * alive
                added = inflow[side, layer, spot, :] * alive
                west_val = rolled(added, 1, 1)
                east_val = rolled(added, -1, 1)
                wet = wet_edge[side, layer, spot, :]
                beyond[1, side, layer] -= wide(1, first) * (pull * added)
                edge_sum[side, KAPPA_NEAR, layer] += adjoint * (wet + (west_val + east_val) - 4.0 * added)
                edge_sum[side, NORTH_NEAR, layer] += swum * wet
                edge_sum[side, EAST_NEAR, layer] += swum * (east_val - west_val)
                edge_sum[side, KAPPA_FAR, layer] += behind * added
                edge_sum[side, NORTH_FAR, layer] += swim * (behind * added)
                edge_sum[side, KAPPA_OWN, layer] += ours * added
                edge_sum[side, NORTH_OWN, layer] += swim * (ours * added)

        over_groups(back2_halo)
        for side in range(2):
            beyond_o[layer, side : side + 1, :] = column(beyond[1, side, layer])
        begin(exchange_beyond(layer))

    def second_pressure(layer):
        summed(2, layer)
        for copy in exchange_beyond(layer):
            copy.wait_recv()
        value = beyond_o[layer]
        for by in range(n_coh - 1):
            value = value + beyond_in[by, layer]
        value = value * (1.0 / every)
        outside[layer] = value
        for side in range(2):
            press_o[side, layer, :1] = total[2, layer, inner(side), :]
            press_o[side, layer, 1:] = value[side : side + 1]
        send(PRESS2, layer)

    def first_back(layer):
        receive(PRESS2, layer)
        total[2, layer] += jnp.where(is_first, press_h[0, layer, 1:], 0.0) + jnp.where(
            is_last, press_h[1, layer, 1:], 0.0
        )

        def inflow_first(first, spot):
            swim = wide(3, first)
            for side in range(2):
                pressure = press_h[side, layer, :1] + outside[layer, side : side + 1]
                adjoint = kept_h[side, layer, spot, :] + wide(2, first) * spread(pressure)
                into[side, layer, spot, :] = coefs[side, layer, spot, :] * adjoint
                product = adjoint * wet1_edge[side, layer, spot, :]
                edge_sum[side, KAPPA_NEAR, layer] += product
                edge_sum[side, NORTH_NEAR, layer] += swim * product

        over_groups(inflow_first)
        for side in range(2):
            for index in range(SENT):
                edge_o[side, layer, index : index + 1] = column(edge_sum[side, index, layer])
        send(EDGE, layer)

        def back1(group, sums):
            added = []
            products = []
            for cohort in group:
                mortal, crowding, weight, swim = scalars(cohort)
                adjoint = kept[cohort, layer] + weight * total[2, layer]
                swum = swim * adjoint
                products.append(
                    (
                        swum * east1[cohort, layer],
                        swum * north1[cohort, layer],
                        adjoint * lap1[cohort, layer],
                    )
                )
                pull = pulled(adjoint, swum, layer, pl.ds(cohort, 1))
                last[cohort, layer] = pull * surv1[cohort, layer]
                added.append(crowding * (pull * wet1[cohort, layer]))
            for index in range(3):
                grads[index, layer] += added_up([product[index] for product in products])
            return sums - added_up(added)

        partial[3, layer] = over_cohorts(back1)
        begin(exchange(3, layer))

    def put(layer):
        return [
            pltpu.make_async_copy(
                last.at[pl.ds(at * chunk, chunk), layer],
                out.at[pl.ds(at * chunk, chunk), layer],
                local_sem.at[2 + layer, at],
            )
            for at in range(CHUNKS)
        ]

    part = lon // n_coh

    def gradients(layer):
        receive(EDGE, layer)
        ocean = field[OCEAN, layer]
        near = (is_first, is_last)
        behind = (row == 1, row == rows - 2)
        drift, climb, kappa = (grads[index, layer] for index in range(3))
        for side in range(2):

            def got(index):
                return edge_h[side, layer, index : index + 1, :]

            sign = -1.0 if side == 0 else 1.0
            kappa_near = got(KAPPA_NEAR) + column(edge_sum[side, KAPPA_OWN, layer])
            north_near = sign * (got(NORTH_NEAR) + column(edge_sum[side, NORTH_OWN, layer]))
            drift = drift + jnp.where(near[side], got(EAST_NEAR), 0.0)
            climb = climb + jnp.where(near[side], north_near, 0.0)
            climb = climb + jnp.where(behind[side], sign * got(NORTH_FAR), 0.0)
            kappa = kappa + jnp.where(near[side], kappa_near, 0.0)
            kappa = kappa + jnp.where(behind[side], got(KAPPA_FAR), 0.0)
        values = (-0.5 * ocean * drift, -0.5 * ocean * climb, ocean * kappa)
        for index, value in enumerate(values):
            for to in range(n_coh):
                share[to, layer, index] = value[:, to * part : (to + 1) * part]
        begin(exchange_share(layer))

    for layer in range(layers):
        first_step(layer)
    for layer in range(layers):
        second_back(layer)
        if layer > 0:
            second_pressure(layer - 1)
        second_beyond(layer)
    for layer in range(layers):
        if layer == layers - 1:
            second_pressure(layer)
        if layer > 0:
            gradients(layer - 1)
        first_back(layer)
        begin(put(layer))
    gradients(layers - 1)
    for layer in range(layers):
        summed(3, layer)
        out_press[layer] = total[3, layer]
        for copy in exchange_share(layer):
            copy.wait_recv()
        for index in range(3):
            value = share[coh, layer, index]
            for by in range(n_coh - 1):
                value = value + share_in[by, layer, index]
            out_grads[index, layer] = value

    for layer in range(layers):
        for copy in put(layer):
            copy.wait()
        for kind in buffers:
            sent(kind, layer)
        for which in range(2 * STEPS):
            for copy in exchange(which, layer):
                copy.wait_send()
        for copy in exchange_beyond(layer) + exchange_share(layer):
            copy.wait_send()


def finish(age, mass, last, press, grads, out, out_east, out_north, out_kappa, held, sem):
    cohorts, layers = held.shape[:2]
    chunk = cohorts // CHUNKS
    spots = [pl.ds(at * chunk, chunk) for at in range(CHUNKS)]
    get = [
        pltpu.make_async_copy(last.at[spot], held.at[spot], sem.at[0, at])
        for at, spot in enumerate(spots)
    ]
    put = [
        pltpu.make_async_copy(held.at[spot], out.at[spot], sem.at[1, at])
        for at, spot in enumerate(spots)
    ]
    for copy in get:
        copy.start()
    for index, target in enumerate((out_east, out_north, out_kappa)):
        target[...] = grads[index]
    for at in range(CHUNKS):
        get[at].wait()
        for cohort in range(at * chunk, (at + 1) * chunk):
            weight = mass[age[cohort]]
            for layer in range(layers):
                held[cohort, layer] += weight * press[layer]
        put[at].start()
    for copy in put:
        copy.wait()


def local(*args):
    density = args[0]
    cohorts, layers, rows, lon = density.shape
    n_lat, n_coh = lax.axis_size("lat"), lax.axis_size("coh")
    f32 = jnp.float32
    vmem = pl.BlockSpec(memory_space=pltpu.VMEM)
    smem = pl.BlockSpec(memory_space=pltpu.SMEM)
    share = jax.ShapeDtypeStruct((layers, rows, lon // n_coh), f32)
    whole = pltpu.VMEM(density.shape, f32)
    packed = pltpu.VMEM((2, layers, cohorts, lon), f32)
    def vec(*shape):
        return pltpu.VMEM(shape, f32)

    part = lon // n_coh
    hbm = pl.BlockSpec(memory_space=pl.ANY)
    scratch = (
        [whole] * 3
        + [
            vec(5, layers, rows, lon),
            vec(2, layers, 10, lon),
            vec(4, cohorts, 128),
        ]
        + [whole] * 7
        + [
            vec(4, layers, rows, lon),
            vec(4, layers, rows, lon),
            vec(4, n_coh - 1, layers, rows, lon),
            vec(3, layers, rows, lon),
            vec(n_coh, layers, 3, rows, part),
            vec(n_coh - 1, layers, 3, rows, part),
            packed,
            vec(2, layers, 8, lon),
            vec(2, layers, 8, lon),
            packed,
            packed,
            packed,
            packed,
            vec(2, layers, 1, lon),
            vec(2, layers, 1, lon),
            vec(2, layers, 1, lon),
            vec(2, layers, 1, lon),
            vec(2, layers, 2, lon),
            vec(2, layers, 2, lon),
            vec(2, layers, SENT, lon),
            vec(2, layers, SENT, lon),
            vec(2, 7, layers, 8, lon),
            vec(2, 2, layers, 8, lon),
            vec(layers, 2, lon),
            vec(n_coh - 1, layers, 2, lon),
            vec(layers, 2, lon),
        ]
        + [packed] * 6
        + [
            pltpu.SemaphoreType.DMA((2 + layers, CHUNKS)),
            pltpu.SemaphoreType.DMA((7, layers, 2)),
            pltpu.SemaphoreType.DMA((7, layers, 2)),
            pltpu.SemaphoreType.DMA((6, layers, n_coh - 1)),
            pltpu.SemaphoreType.DMA((6, layers, n_coh - 1)),
        ]
    )
    size = density.size
    last, press, grads = pl.pallas_call(
        functools.partial(kernel, n_lat, n_coh),
        out_shape=(
            jax.ShapeDtypeStruct(density.shape, f32),
            jax.ShapeDtypeStruct((layers, rows, lon), f32),
            jax.ShapeDtypeStruct((3, layers, rows, part), f32),
        ),
        in_specs=[hbm] * 2 + [vmem] * 4 + [smem] * 5,
        out_specs=(hbm, vmem, vmem),
        scratch_shapes=scratch,
        compiler_params=pltpu.CompilerParams(
            collective_id=0, has_side_effects=True, vmem_limit_bytes=56 * 1024 * 1024
        ),
        cost_estimate=pl.CostEstimate(
            flops=150 * size, bytes_accessed=12 * size, transcendentals=2 * size
        ),
    )(*args)
    return pl.pallas_call(
        finish,
        out_shape=(jax.ShapeDtypeStruct(density.shape, f32), share, share, share),
        in_specs=[smem, smem, hbm, vmem, vmem],
        out_specs=(hbm, vmem, vmem, vmem),
        scratch_shapes=[whole, pltpu.SemaphoreType.DMA((2, CHUNKS))],
        compiler_params=pltpu.CompilerParams(vmem_limit_bytes=56 * 1024 * 1024),
        cost_estimate=pl.CostEstimate(flops=2 * size, bytes_accessed=8 * size, transcendentals=0),
    )(args[6], args[9], last, press, grads)


def solution(mesh):
    fields = P(None, "lat", None)
    in_specs = (P("coh", None, "lat", None),) * 2 + (fields,) * 4 + (P("coh"),) + (P(),) * 4
    out_specs = (P("coh", None, "lat", None),) + (P(None, "lat", "coh"),) * 3
    return jax.shard_map(local, mesh=mesh, in_specs=in_specs, out_specs=out_specs, check_vma=False)
```

time: 278 us -> 62.4 us (0.22)
  waiting for transfers between devices: 174 us -> 0 us
  Pallas kernels: 0 us -> 61.5 us
  other arithmetic: 41.2 us -> 0 us
  local copies, waits for them, and re-layouts: 23.9 us -> 0 us
  starting transfers between devices: 23.1 us -> 0 us
  between operations: 14.6 us -> 0.64 us
    psum x4 -> x0, waiting for transfers between devices: 98.3 us -> none  [the longest x2 54.1 us: local(): lax.psum(jnp.sum(-crowding * grad_surv * survived, axis=0), 'coh')]
    reduce_scatter x3 -> x0, waiting for transfers between devices: 63.3 us -> none  [the longest x1 22.5 us: local(): lax.psum_scatter(grad_north, 'coh', scatter_dimension=2, tiled=True)]
    pallas_call x0 -> x2, Pallas kernels: none -> 61.5 us  [the longest x1 57.6 us: local(): pl.pallas_call(functools.partial(kernel, n_lat, n_coh), out_shape=(jax.Sh...]
    reduce_sum x5 -> x0, other arithmetic: 24 us -> none  [the longest x2 11.2 us: local(): jnp.sum(-crowding * grad_surv * survived, axis=0)]
    ppermute x8 -> x0, starting transfers between devices: 22.9 us -> none  [the longest x4 11.3 us: passed_along(): return lax.ppermute(value, axis, pairs)]
    slice x20 -> x0, local copies, waits for them, and re-layouts: 20.5 us -> none  [the longest x4 5.55 us: local(): east_val = jnp.roll(wet, -1, axis=3)]
    ppermute x8 -> x0, waiting for transfers between devices: 12.2 us -> none  [the longest x2 5.77 us: extended(): before = lax.ppermute(last, axis, up)]
    mul x3 -> x0, other arithmetic: 11.1 us -> none  [the longest x2 8.11 us: local(): to_east = (kappa - 0.5 * east_coef) * masked]
  transfers between devices with their start and end apart: 15 -> 0, of which waited for: 10 -> 0; matrix products, arithmetic and copies ran while one was open for 13% -> 0% of each run, Pallas kernels for 0% -> 0%
where the time goes in v3:
time: 62.4 us; the launch traced here: 62.2 us
  Pallas kernels  61.5 us (99%)
  between operations  0.64 us (1%)
    pallas_call x1, Pallas kernels, local(): pl.pallas_call(functools.partial(kernel, n_lat, n_coh), out_shape=(jax.Sh...  57.6 us
    pallas_call x1, Pallas kernels, local(): pl.pallas_call(finish, out_shape=(jax.ShapeDtypeStruct(density.shape, f32...  3.9 us

profile of v3, /device:TPU:0, one launch (start us, length us, event | category | flops | bytes accessed | tf_op | source)
XLA Modules:
  0.0 62.2 jit_solution(9447906750698903736)
XLA Ops:
  0.6 57.6 %shard_map.138 = (f32[32,2,8,1024]{3,2,1,0:T(8,128)}, f32[2,8,1024]{2,1,0:T(8,128)}, f32[3,2,8,256]{3,2,1,0:T(8,128)}) custom-call(f32[32,2,8,1024]{3,2,1,0:T(8,128)} %dens_in.1, f32[32,2,8,1024]{3,2,1,0:T(8,128)} %cot_in.1, s32[2,8,1024]{2,1,0:T(8,128)} %land.1, f32[2,8,1024]{2,1,0:T(8,128)} %east.1, f32[2,8,1024]{2,1,0:T(8,128)} %north.1, ...), custom_call_target="tpu_custom_call" | custom-call | flops 78643200 | bytes 6291456 | tf_op jit(solution)/shard_map/pallas_call | solution.py:760
  58.3 3.9 %shard_map.139 = (f32[32,2,8,1024]{3,2,1,0:T(8,128)}, f32[2,8,256]{2,1,0:T(8,128)}, f32[2,8,256]{2,1,0:T(8,128)}, f32[2,8,256]{2,1,0:T(8,128)}) custom-call(s32[32]{0:T(128)} %age.3, f32[32]{0:T(128)} %mass.3, f32[32,2,8,1024]{3,2,1,0:T(8,128)} %get-tuple-element.7.last, f32[2,8,1024]{2,1,0:T(8,128)} %get-tuple-element.8.press, ...), custom_call_target="tpu_custom_call" | custom-call | flops 1048576 | bytes 4194304 | tf_op jit(solution)/shard_map/pallas_call | solution.py:777

commit v4 on v3

--- a/solution.py
+++ b/solution.py
@@ -12,9 +12,11 @@
 FIELDS, COT1, COT2, PART2, CROWD2, PRESS2, EDGE = range(7)
 KAPPA_NEAR, NORTH_NEAR, EAST_NEAR, KAPPA_FAR, NORTH_FAR, KAPPA_OWN, NORTH_OWN = range(7)
 SENT = 5
-GROUP = 4
+GROUP = 16
+LANES = 128
 CHUNKS = 8
 CENTRE, KAPPA, EAST, NORTH, OCEAN = range(5)
+KAPPA_W, KAPPA_E, KAPPA_S, KAPPA_N, EAST_W, EAST_E, NORTH_S, NORTH_N = range(5, 13)
 
 
 def rolled(value, by, axis):
@@ -47,6 +49,8 @@
     state,
     surv1,
     wet1,
+    surv2,
+    wet2,
     lap1,
     east1,
     north1,
@@ -73,16 +77,16 @@
     edge_o,
     edge_h,
     edge_sum,
-    beyond,
     beyond_o,
     beyond_in,
     outside,
     wet_edge,
     wet1_edge,
-    coefs,
     inflow,
-    into,
+    adj_h,
     kept_h,
+    alive_h,
+    added_h,
     local_sem,
     lat_send,
     lat_recv,
@@ -265,26 +269,51 @@
     for copy in get_dens:
         copy.wait()
 
-    zero = jnp.zeros((rows, lon), jnp.float32)
-
-    def over_cohorts(body):
+    chunks = lon // LANES
+    lane = lax.broadcasted_iota(jnp.int32, (8, LANES), 1)
+    leftmost = lane == 0
+    rightmost = lane == LANES - 1
+    row = lax.broadcasted_iota(jnp.int32, (rows, LANES), 0)
+    is_first = row == 0
+    is_last = row == rows - 1
+    zero = jnp.zeros((rows, LANES), jnp.float32)
+
+    def lanes_of(at):
+        return pl.ds(pl.multiple_of(at * LANES, LANES), LANES)
+
+    def over_chunks(body):
+        def one(at, carry):
+            west, east = lax.rem(at + (chunks - 1), chunks), lax.rem(at + 1, chunks)
+            body(lanes_of(at), lanes_of(west), lanes_of(east))
+            return carry
+
+        lax.fori_loop(0, chunks, one, 0)
+
+    def over_cohorts(body, carry):
         def one(step, carry):
-            return body([step * GROUP + member for member in range(GROUP)], carry)
-
-        return lax.fori_loop(0, cohorts // GROUP, one, zero)
-
-    def added_up(values):
-        value = values[0]
-        for other in values[1:]:
-            value = value + other
-        return value
-
-    for layer in range(layers):
-
-        def weigh(group, sums, layer=layer):
-            return sums + added_up([mass[age[cohort]] * dens[cohort, layer] for cohort in group])
-
-        partial[0, layer] = over_cohorts(weigh)
+            first = pl.multiple_of(step * GROUP, 8)
+            for member in range(GROUP):
+                eight = pl.ds(pl.multiple_of(first + member // 8 * 8, 8), 8)
+                carry = body(first + member, (eight, member % 8), carry)
+            return carry
+
+        return lax.fori_loop(0, cohorts // GROUP, one, carry)
+
+    def at_west(here, west):
+        return pltpu.roll(jnp.where(rightmost, west, here), 1, 1)
+
+    def at_east(here, east):
+        return pltpu.roll(jnp.where(leftmost, east, here), LANES - 1, 1)
+
+    for layer in range(layers):
+
+        def weigh_chunk(here, west, east, layer=layer):
+            def weigh(cohort, spot, sums):
+                return sums + mass[age[cohort]] * dens[cohort, layer, :, here]
+
+            partial[0, layer, :, here] = over_cohorts(weigh, zero)
+
+        over_chunks(weigh_chunk)
         begin(exchange(0, layer))
 
     for layer in range(layers):
@@ -309,27 +338,23 @@
         send(COT2, layer)
     for layer in range(layers):
         pack(dens, layer, 0, rows - 1, dens_edge)
-    grads[...] = jnp.zeros(grads.shape, jnp.float32)
-    edge_sum[...] = jnp.zeros(edge_sum.shape, jnp.float32)
-    beyond[...] = jnp.zeros(beyond.shape, jnp.float32)
 
     def wide(index, first):
-        value = params[index, pl.ds(first, 8), :]
-        return jnp.concatenate([value] * (lon // 128), axis=1)
-
-    def spread(row):
-        return jnp.broadcast_to(row, (8, lon))
-
-    def over_groups(body):
-        def one(group, carry):
-            first = pl.multiple_of(group * 8, 8)
-            body(first, pl.ds(first, 8))
-            return carry
-
-        lax.fori_loop(0, cohorts // 8, one, 0)
-
-    def halo_row(side, index, depth, layer):
-        return spread(halo_field[side, layer, 2 * index + depth : 2 * index + depth + 1, :])
+        return params[index, first : first + 8, :]
+
+    def over_edges(body):
+        def one(here, west, east):
+            for side in range(2):
+                body(side, here, west, east)
+
+        over_chunks(one)
+
+    def spread(value):
+        return jnp.broadcast_to(value, (8, LANES))
+
+    def halo_row(side, index, depth, layer, here):
+        spot = 2 * index + depth if index < 5 else index + 5
+        return spread(halo_field[side, layer, spot : spot + 1, here])
 
     for layer in range(layers):
         receive(FIELDS, layer)
@@ -345,10 +370,23 @@
             )
             for index, value in enumerate(values):
                 halo_field[side, layer, 2 * index : 2 * index + 2] = value
-
-    def survival_h(side, first, layer):
-        crowd = spread(crowd_h[side, layer])
-        return halo_row(side, OCEAN, 0, layer) * jnp.exp(-(wide(0, first) + wide(1, first) * crowd))
+            near = [value[:1] for value in values]
+            for index, by in ((KAPPA_W, 1), (KAPPA_E, -1), (EAST_W, 1), (EAST_E, -1)):
+                base = near[KAPPA] if index in (KAPPA_W, KAPPA_E) else near[EAST]
+                halo_field[side, layer, index + 5 : index + 6] = rolled(base, by, 1)
+        kappa, drift, climb = field[KAPPA, layer], field[EAST, layer], field[NORTH, layer]
+        field[KAPPA_W, layer] = rolled(kappa, 1, 1)
+        field[KAPPA_E, layer] = rolled(kappa, -1, 1)
+        field[EAST_W, layer] = rolled(drift, 1, 1)
+        field[EAST_E, layer] = rolled(drift, -1, 1)
+        field[KAPPA_S, layer] = rolled(kappa, 1, 0)
+        field[KAPPA_N, layer] = rolled(kappa, -1, 0)
+        field[NORTH_S, layer] = rolled(climb, 1, 0)
+        field[NORTH_N, layer] = rolled(climb, -1, 0)
+        for index, origin in ((KAPPA_S, KAPPA), (NORTH_S, NORTH)):
+            field[index, layer, :1] = halo_field[0, layer, 2 * origin : 2 * origin + 1]
+        for index, origin in ((KAPPA_N, KAPPA), (NORTH_N, NORTH)):
+            field[index, layer, rows - 1 :] = halo_field[1, layer, 2 * origin : 2 * origin + 1]
 
     def inner(side):
         return slice(0, 1) if side == 0 else slice(rows - 1, rows)
@@ -356,182 +394,223 @@
     def column(value):
         return jnp.sum(value, axis=0, keepdims=True)
 
-    row = lax.broadcasted_iota(jnp.int32, (rows, lon), 0)
-    is_first = row == 0
-    is_last = row == rows - 1
-
     def from_before(value, edge):
         return jnp.where(is_first, edge, rolled(value, 1, 0))
 
     def from_after(value, edge):
         return jnp.where(is_last, edge, rolled(value, -1, 0))
 
-    def scalars(cohort):
-        one = age[cohort]
-        return mort[one], crowd_coef[one], mass[one], speed[one]
-
-    def survival(layer, which, mortal, crowding):
-        return field[OCEAN, layer] * jnp.exp(-(mortal + crowding * total[which, layer]))
+    def edge_row(ref, side, layer, spot, here):
+        eight, member = spot
+        return ref[side, layer, eight, here][member : member + 1]
+
+    def whole_rows(first_edge, last_edge):
+        full = lax.broadcasted_iota(jnp.int32, (rows, lon), 0)
+        return jnp.where(full == 0, first_edge, 0.0) + jnp.where(full == rows - 1, last_edge, 0.0)
+
+    def survive(layer, which, start, alive_ref, wet_ref, edges):
+        def one(here, west, east):
+            ocean = field[OCEAN, layer, :, here]
+            crowd = total[which, layer, :, here]
+            held = []
+
+            def each(cohort, spot, carry):
+                age_of = age[cohort]
+                alive = ocean * jnp.exp(-(mort[age_of] + crowd_coef[age_of] * crowd))
+                wet = start[cohort, layer, :, here] * alive
+                alive_ref[cohort, layer, :, here] = alive
+                wet_ref[cohort, layer, :, here] = wet
+                if edges:
+                    eight, member = spot
+                    if member == 0:
+                        held.clear()
+                    held.append(wet)
+                    if member == 7:
+                        for side in range(2):
+                            edge = [value[inner(side)] for value in held]
+                            wet_edge[side, layer, eight, here] = jnp.concatenate(edge, axis=0)
+                return carry
+
+            over_cohorts(each, 0)
+
+        over_chunks(one)
 
     def first_step(layer):
         summed(0, layer)
 
-        def outflow(first, spot):
-            swim = wide(3, first)
-            for side in range(2):
-                crowd = spread(total[0, layer, inner(side), :])
-                ocean = spread(field[OCEAN, layer, inner(side), :])
+        def outflow(side, here, west, east):
+            crowd = spread(total[0, layer, inner(side), here])
+            ocean = spread(field[OCEAN, layer, inner(side), here])
+            climb = halo_row(side, NORTH, 0, layer, here)
+            kappa = halo_row(side, KAPPA, 0, layer, here)
+            sums = jnp.zeros((8, LANES), jnp.float32)
+            for first in range(0, cohorts, 8):
+                spot = pl.ds(first, 8)
                 alive = ocean * jnp.exp(-(wide(0, first) + wide(1, first) * crowd))
-                wet = dens_edge[side, layer, spot, :] * alive
-                shift = swim * halo_row(side, NORTH, 0, layer)
-                kappa = halo_row(side, KAPPA, 0, layer)
+                wet = dens_edge[side, layer, spot, here] * alive
+                shift = wide(3, first) * climb
                 coef = kappa - shift if side == 0 else kappa + shift
                 value = coef * wet
-                wet1_edge[side, layer, spot, :] = wet
-                coefs[side, layer, spot, :] = coef
-                inflow[side, layer, spot, :] = value
-                beyond[0, side, layer] += wide(2, first) * value
-
-        over_groups(outflow)
-        for side in range(2):
-            part_o[side, layer] = column(beyond[0, side, layer])
+                wet1_edge[side, layer, spot, here] = wet
+                inflow[side, layer, spot, here] = value
+                sums = sums + wide(2, first) * value
+            part_o[side, layer, :, here] = column(sums)
+
+        over_edges(outflow)
         send(PART2, layer)
-
-        def forward(group, sums):
-            added = []
-            for cohort in group:
-                mortal, crowding, weight, swim = scalars(cohort)
-                alive = survival(layer, 0, mortal, crowding)
-                wet = dens[cohort, layer] * alive
+        survive(layer, 0, dens, surv1, wet1, False)
+
+        def forward_chunk(here, west, east):
+            centre, kappa, drift, climb = (field[index, layer, :, here] for index in range(4))
+
+            def forward(cohort, spot, sums):
+                age_of = age[cohort]
+                wet = wet1[cohort, layer, :, here]
+                west_val = at_west(wet, wet1[cohort, layer, :, west])
+                east_val = at_east(wet, wet1[cohort, layer, :, east])
                 before = from_before(wet, 0.0)
                 after = from_after(wet, 0.0)
-                west_val = rolled(wet, 1, 1)
-                east_val = rolled(wet, -1, 1)
                 around = (before + after) + (west_val + east_val)
                 east_diff = east_val - west_val
                 north_diff = after - before
-                value = (
-                    field[CENTRE, layer] * wet
-                    + field[KAPPA, layer] * around
-                    - swim * (field[EAST, layer] * east_diff + field[NORTH, layer] * north_diff)
+                value = (centre * wet + kappa * around) - speed[age_of] * (
+                    drift * east_diff + climb * north_diff
                 )
-                surv1[cohort, layer] = alive
-                wet1[cohort, layer] = wet
-                lap1[cohort, layer] = around - 4.0 * wet
-                east1[cohort, layer] = east_diff
-                north1[cohort, layer] = north_diff
-                state[cohort, layer] = value
-                added.append(weight * value)
-            return sums + added_up(added)
-
-        sums = over_cohorts(forward)
+                lap1[cohort, layer, :, here] = around - 4.0 * wet
+                east1[cohort, layer, :, here] = east_diff
+                north1[cohort, layer, :, here] = north_diff
+                state[cohort, layer, :, here] = value
+                return sums + mass[age_of] * value
+
+            partial[1, layer, :, here] = over_cohorts(forward, zero)
+
+        over_chunks(forward_chunk)
         receive(PART2, layer)
-        partial[1, layer] = sums + (
-            jnp.where(is_first, part_h[0, layer], 0.0) + jnp.where(is_last, part_h[1, layer], 0.0)
+        partial[1, layer] += whole_rows(part_h[0, layer], part_h[1, layer])
+        begin(exchange(1, layer))
+
+    def pulled(coefs, swim, here, west, east, south, north):
+        return (
+            coefs[0] * here
+            + (coefs[1] * west + coefs[2] * east)
+            + (coefs[3] * south + coefs[4] * north)
+            - swim * ((coefs[5] * west - coefs[6] * east) + (coefs[7] * south - coefs[8] * north))
         )
-        begin(exchange(1, layer))
-
-    def pulled(adjoint, swum, layer, spot):
-        spread_out = field[KAPPA, layer] * adjoint
-        drift = field[EAST, layer] * swum
-        climb = field[NORTH, layer] * swum
-        return (
-            field[CENTRE, layer] * adjoint
-            + rolled(spread_out - drift, 1, 1)
-            + rolled(spread_out + drift, -1, 1)
-            + from_before(spread_out - climb, into[0, layer, spot, :])
-            + from_after(spread_out + climb, into[1, layer, spot, :])
-        )
+
+    def gathered(layer, here):
+        indices = (CENTRE, KAPPA_W, KAPPA_E, KAPPA_S, KAPPA_N, EAST_W, EAST_E, NORTH_S, NORTH_N)
+        return [field[index, layer, :, here] for index in indices]
 
     def second_back(layer):
-        receive(COT1, layer)
-
-        def inflow_cot(first, spot):
-            for side in range(2):
-                into[side, layer, spot, :] = coefs[side, layer, spot, :] * cot1_h[side, layer, spot, :]
-
-        over_groups(inflow_cot)
         summed(1, layer)
         for side in range(2):
             crowd_o[side, layer] = total[1, layer, inner(side), :]
         send(CROWD2, layer)
-
-        def back2(group, sums):
-            added = []
-            products = []
-            for cohort in group:
-                mortal, crowding, weight, swim = scalars(cohort)
-                spot = pl.ds(cohort, 1)
-                alive = survival(layer, 1, mortal, crowding)
-                wet = state[cohort, layer] * alive
-                wet_edge[0, layer, spot, :] = wet[:1]
-                wet_edge[1, layer, spot, :] = wet[rows - 1 :]
+        survive(layer, 1, state, surv2, wet2, True)
+        receive(COT1, layer)
+
+        def back2_chunk(here, west, east):
+            coefs = gathered(layer, here)
+
+            def back2(cohort, spot, sums):
+                age_of = age[cohort]
+                swim = speed[age_of]
+                wet = wet2[cohort, layer, :, here]
+                west_val = at_west(wet, wet2[cohort, layer, :, west])
+                east_val = at_east(wet, wet2[cohort, layer, :, east])
                 before = from_before(wet, 0.0)
                 after = from_after(wet, 0.0)
-                west_val = rolled(wet, 1, 1)
-                east_val = rolled(wet, -1, 1)
-                adjoint = cot[cohort, layer]
+                adjoint = cot[cohort, layer, :, here]
                 swum = swim * adjoint
-                products.append(
-                    (
-                        swum * (east_val - west_val),
-                        swum * (after - before),
-                        adjoint * ((before + after) + (west_val + east_val) - 4.0 * wet),
-                    )
+                pull = pulled(
+                    coefs,
+                    swim,
+                    adjoint,
+                    at_west(adjoint, cot[cohort, layer, :, west]),
+                    at_east(adjoint, cot[cohort, layer, :, east]),
+                    from_before(adjoint, edge_row(cot1_h, 0, layer, spot, here)),
+                    from_after(adjoint, edge_row(cot1_h, 1, layer, spot, here)),
                 )
-                pull = pulled(adjoint, swum, layer, spot)
-                kept[cohort, layer] = pull * alive
-                added.append(crowding * (pull * wet))
+                kept[cohort, layer, :, here] = pull * surv2[cohort, layer, :, here]
+                return (
+                    sums[0] + swum * (east_val - west_val),
+                    sums[1] + swum * (after - before),
+                    sums[2] + adjoint * ((before + after) + (west_val + east_val) - 4.0 * wet),
+                    sums[3] - crowd_coef[age_of] * (pull * wet),
+                )
+
+            sums = over_cohorts(back2, (zero,) * 4)
             for index in range(3):
-                grads[index, layer] += added_up([product[index] for product in products])
-            return sums - added_up(added)
-
-        partial[2, layer] = over_cohorts(back2)
+                grads[index, layer, :, here] = sums[index]
+            partial[2, layer, :, here] = sums[3]
+
+        over_chunks(back2_chunk)
         begin(exchange(2, layer))
 
     def second_beyond(layer):
         receive(CROWD2, layer)
+
+        def survive_halo(side, here, west, east):
+            crowd = spread(crowd_h[side, layer, :, here])
+            ocean = halo_row(side, OCEAN, 0, layer, here)
+            for first in range(0, cohorts, 8):
+                spot = pl.ds(first, 8)
+                alive = ocean * jnp.exp(-(wide(0, first) + wide(1, first) * crowd))
+                alive_h[side, layer, spot, here] = alive
+                added_h[side, layer, spot, here] = inflow[side, layer, spot, here] * alive
+
+        over_edges(survive_halo)
         receive(COT2, layer)
 
-        def back2_halo(first, spot):
-            swim = wide(3, first)
-            for side in range(2):
-                sign = 1.0 if side == 0 else -1.0
-                adjoint = cot1_h[side, layer, spot, :]
-                behind = cot2_h[side, layer, spot, :]
-                ours = cot1_o[side, layer, spot, :]
+        def back2_halo(side, here, west, east):
+            sign = 1.0 if side == 0 else -1.0
+            centre, kappa_w, kappa_e, drift_w, drift_e = (
+                halo_row(side, index, 0, layer, here)
+                for index in (CENTRE, KAPPA_W, KAPPA_E, EAST_W, EAST_E)
+            )
+            outer_kappa = halo_row(side, KAPPA, 1, layer, here)
+            outer_climb = sign * halo_row(side, NORTH, 1, layer, here)
+            inner_kappa = spread(field[KAPPA, layer, inner(side), here])
+            inner_climb = sign * spread(field[NORTH, layer, inner(side), here])
+            sums = [jnp.zeros((8, LANES), jnp.float32)] * 8
+            for first in range(0, cohorts, 8):
+                spot = pl.ds(first, 8)
+                swim = wide(3, first)
+                adjoint = cot1_h[side, layer, spot, here]
+                behind = cot2_h[side, layer, spot, here]
+                ours = cot1_o[side, layer, spot, here]
+                adj_w = at_west(adjoint, cot1_h[side, layer, spot, west])
+                adj_e = at_east(adjoint, cot1_h[side, layer, spot, east])
+                pull = (
+                    centre * adjoint
+                    + (kappa_w * adj_w + kappa_e * adj_e)
+                    + (outer_kappa * behind + inner_kappa * ours)
+                    - swim
+                    * ((drift_w * adj_w - drift_e * adj_e) + (outer_climb * behind - inner_climb * ours))
+                )
+                kept_h[side, layer, spot, here] = pull * alive_h[side, layer, spot, here]
+                added = added_h[side, layer, spot, here]
+                west_val = at_west(added, added_h[side, layer, spot, west])
+                east_val = at_east(added, added_h[side, layer, spot, east])
+                wet = wet_edge[side, layer, spot, here]
                 swum = swim * adjoint
-                spread_out = halo_row(side, KAPPA, 0, layer) * adjoint
-                drift = halo_row(side, EAST, 0, layer) * swum
-                outer_coef = halo_row(side, KAPPA, 1, layer) - sign * swim * halo_row(side, NORTH, 1, layer)
-                inner_coef = spread(field[KAPPA, layer, inner(side), :]) + sign * swim * spread(
-                    field[NORTH, layer, inner(side), :]
-                )
-                pull = (
-                    halo_row(side, CENTRE, 0, layer) * adjoint
-                    + rolled(spread_out - drift, 1, 1)
-                    + rolled(spread_out + drift, -1, 1)
-                    + outer_coef * behind
-                    + inner_coef * ours
-                )
-                alive = survival_h(side, first, layer)
-                kept_h[side, layer, spot, :] = pull * alive
-                added = inflow[side, layer, spot, :] * alive
-                west_val = rolled(added, 1, 1)
-                east_val = rolled(added, -1, 1)
-                wet = wet_edge[side, layer, spot, :]
-                beyond[1, side, layer] -= wide(1, first) * (pull * added)
-                edge_sum[side, KAPPA_NEAR, layer] += adjoint * (wet + (west_val + east_val) - 4.0 * added)
-                edge_sum[side, NORTH_NEAR, layer] += swum * wet
-                edge_sum[side, EAST_NEAR, layer] += swum * (east_val - west_val)
-                edge_sum[side, KAPPA_FAR, layer] += behind * added
-                edge_sum[side, NORTH_FAR, layer] += swim * (behind * added)
-                edge_sum[side, KAPPA_OWN, layer] += ours * added
-                edge_sum[side, NORTH_OWN, layer] += swim * (ours * added)
-
-        over_groups(back2_halo)
-        for side in range(2):
-            beyond_o[layer, side : side + 1, :] = column(beyond[1, side, layer])
+                far, own = behind * added, ours * added
+                for index, value in (
+                    (KAPPA_NEAR, adjoint * (wet + (west_val + east_val) - 4.0 * added)),
+                    (NORTH_NEAR, swum * wet),
+                    (EAST_NEAR, swum * (east_val - west_val)),
+                    (KAPPA_FAR, far),
+                    (NORTH_FAR, swim * far),
+                    (KAPPA_OWN, own),
+                    (NORTH_OWN, swim * own),
+                    (7, wide(1, first) * (pull * added)),
+                ):
+                    sums[index] = sums[index] + value
+            for index in range(7):
+                edge_sum[side, layer, index : index + 1, here] = column(sums[index])
+            beyond_o[layer, side : side + 1, here] = -column(sums[7])
+
+        over_edges(back2_halo)
         begin(exchange_beyond(layer))
 
     def second_pressure(layer):
@@ -550,48 +629,63 @@
 
     def first_back(layer):
         receive(PRESS2, layer)
-        total[2, layer] += jnp.where(is_first, press_h[0, layer, 1:], 0.0) + jnp.where(
-            is_last, press_h[1, layer, 1:], 0.0
-        )
-
-        def inflow_first(first, spot):
-            swim = wide(3, first)
-            for side in range(2):
-                pressure = press_h[side, layer, :1] + outside[layer, side : side + 1]
-                adjoint = kept_h[side, layer, spot, :] + wide(2, first) * spread(pressure)
-                into[side, layer, spot, :] = coefs[side, layer, spot, :] * adjoint
-                product = adjoint * wet1_edge[side, layer, spot, :]
-                edge_sum[side, KAPPA_NEAR, layer] += product
-                edge_sum[side, NORTH_NEAR, layer] += swim * product
-
-        over_groups(inflow_first)
-        for side in range(2):
+        total[2, layer] += whole_rows(press_h[0, layer, 1:], press_h[1, layer, 1:])
+
+        def inflow_first(side, here, west, east):
+            pressure = spread(press_h[side, layer, :1, here] + outside[layer, side : side + 1, here])
+            sums = [jnp.zeros((8, LANES), jnp.float32)] * 2
+            for first in range(0, cohorts, 8):
+                spot = pl.ds(first, 8)
+                adjoint = kept_h[side, layer, spot, here] + wide(2, first) * pressure
+                adj_h[side, layer, spot, here] = adjoint
+                product = adjoint * wet1_edge[side, layer, spot, here]
+                sums = [sums[0] + product, sums[1] + wide(3, first) * product]
             for index in range(SENT):
-                edge_o[side, layer, index : index + 1] = column(edge_sum[side, index, layer])
+                value = edge_sum[side, layer, index : index + 1, here]
+                if index in (KAPPA_NEAR, NORTH_NEAR):
+                    value = value + column(sums[index])
+                edge_o[side, layer, index : index + 1, here] = value
+
+        over_edges(inflow_first)
         send(EDGE, layer)
 
-        def back1(group, sums):
-            added = []
-            products = []
-            for cohort in group:
-                mortal, crowding, weight, swim = scalars(cohort)
-                adjoint = kept[cohort, layer] + weight * total[2, layer]
+        def back1_chunk(here, west, east):
+            coefs = gathered(layer, here)
+            press = total[2, layer, :, here]
+            press_w = jnp.where(rightmost, total[2, layer, :, west], press)
+            press_e = jnp.where(leftmost, total[2, layer, :, east], press)
+
+            def back1(cohort, spot, sums):
+                age_of = age[cohort]
+                swim, weight = speed[age_of], mass[age_of]
+                held = kept[cohort, layer, :, here]
+                adjoint = held + weight * press
+                adj_w = jnp.where(rightmost, kept[cohort, layer, :, west], held) + weight * press_w
+                adj_e = jnp.where(leftmost, kept[cohort, layer, :, east], held) + weight * press_e
                 swum = swim * adjoint
-                products.append(
-                    (
-                        swum * east1[cohort, layer],
-                        swum * north1[cohort, layer],
-                        adjoint * lap1[cohort, layer],
-                    )
+                pull = pulled(
+                    coefs,
+                    swim,
+                    adjoint,
+                    pltpu.roll(adj_w, 1, 1),
+                    pltpu.roll(adj_e, LANES - 1, 1),
+                    from_before(adjoint, edge_row(adj_h, 0, layer, spot, here)),
+                    from_after(adjoint, edge_row(adj_h, 1, layer, spot, here)),
                 )
-                pull = pulled(adjoint, swum, layer, pl.ds(cohort, 1))
-                last[cohort, layer] = pull * surv1[cohort, layer]
-                added.append(crowding * (pull * wet1[cohort, layer]))
+                last[cohort, layer, :, here] = pull * surv1[cohort, layer, :, here]
+                return (
+                    sums[0] + swum * east1[cohort, layer, :, here],
+                    sums[1] + swum * north1[cohort, layer, :, here],
+                    sums[2] + adjoint * lap1[cohort, layer, :, here],
+                    sums[3] - crowd_coef[age_of] * (pull * wet1[cohort, layer, :, here]),
+                )
+
+            sums = over_cohorts(back1, (zero,) * 4)
             for index in range(3):
-                grads[index, layer] += added_up([product[index] for product in products])
-            return sums - added_up(added)
-
-        partial[3, layer] = over_cohorts(back1)
+                grads[index, layer, :, here] += sums[index]
+            partial[3, layer, :, here] = sums[3]
+
+        over_chunks(back1_chunk)
         begin(exchange(3, layer))
 
     def put(layer):
@@ -609,17 +703,21 @@
     def gradients(layer):
         receive(EDGE, layer)
         ocean = field[OCEAN, layer]
-        near = (is_first, is_last)
-        behind = (row == 1, row == rows - 2)
+        full = lax.broadcasted_iota(jnp.int32, (rows, lon), 0)
+        near = (full == 0, full == rows - 1)
+        behind = (full == 1, full == rows - 2)
         drift, climb, kappa = (grads[index, layer] for index in range(3))
         for side in range(2):
 
             def got(index):
                 return edge_h[side, layer, index : index + 1, :]
 
+            def own(index):
+                return edge_sum[side, layer, index : index + 1, :]
+
             sign = -1.0 if side == 0 else 1.0
-            kappa_near = got(KAPPA_NEAR) + column(edge_sum[side, KAPPA_OWN, layer])
-            north_near = sign * (got(NORTH_NEAR) + column(edge_sum[side, NORTH_OWN, layer]))
+            kappa_near = got(KAPPA_NEAR) + own(KAPPA_OWN)
+            north_near = sign * (got(NORTH_NEAR) + own(NORTH_OWN))
             drift = drift + jnp.where(near[side], got(EAST_NEAR), 0.0)
             climb = climb + jnp.where(near[side], north_near, 0.0)
             climb = climb + jnp.where(behind[side], sign * got(NORTH_FAR), 0.0)
@@ -714,11 +812,11 @@
     scratch = (
         [whole] * 3
         + [
-            vec(5, layers, rows, lon),
-            vec(2, layers, 10, lon),
+            vec(13, layers, rows, lon),
+            vec(2, layers, 18, lon),
             vec(4, cohorts, 128),
         ]
-        + [whole] * 7
+        + [whole] * 9
         + [
             vec(4, layers, rows, lon),
             vec(4, layers, rows, lon),
@@ -741,13 +839,12 @@
             vec(2, layers, 2, lon),
             vec(2, layers, SENT, lon),
             vec(2, layers, SENT, lon),
-            vec(2, 7, layers, 8, lon),
-            vec(2, 2, layers, 8, lon),
+            vec(2, layers, 7, lon),
             vec(layers, 2, lon),
             vec(n_coh - 1, layers, 2, lon),
             vec(layers, 2, lon),
         ]
-        + [packed] * 6
+        + [packed] * 7
         + [
             pltpu.SemaphoreType.DMA((2 + layers, CHUNKS)),
             pltpu.SemaphoreType.DMA((7, layers, 2)),

time: 62.4 us -> 65.4 us (1.048)
  Pallas kernels: 61.5 us -> 64.5 us
    pallas_call x1, Pallas kernels: 57.6 us -> 60.6 us  [local(): pl.pallas_call(functools.partial(kernel, n_lat, n_coh), out_shape=(jax.Sh...]
where the time goes in v4:
time: 65.4 us; the launch traced here: 65.2 us
  Pallas kernels  64.5 us (99%)
    pallas_call x1, Pallas kernels, local(): pl.pallas_call(functools.partial(kernel, n_lat, n_coh), out_shape=(jax.Sh...  60.6 us
    pallas_call x1, Pallas kernels, local(): pl.pallas_call(finish, out_shape=(jax.ShapeDtypeStruct(density.shape, f32...  3.9 us

profile of v4, /device:TPU:0, one launch (start us, length us, event | category | flops | bytes accessed | tf_op | source)
XLA Modules:
  0.0 65.2 jit_solution(5254759206540732625)
XLA Ops:
  0.6 60.6 %shard_map.138 = (f32[32,2,8,1024]{3,2,1,0:T(8,128)}, f32[2,8,1024]{2,1,0:T(8,128)}, f32[3,2,8,256]{3,2,1,0:T(8,128)}) custom-call(f32[32,2,8,1024]{3,2,1,0:T(8,128)} %dens_in.1, f32[32,2,8,1024]{3,2,1,0:T(8,128)} %cot_in.1, s32[2,8,1024]{2,1,0:T(8,128)} %land.1, f32[2,8,1024]{2,1,0:T(8,128)} %east.1, f32[2,8,1024]{2,1,0:T(8,128)} %north.1, ...), custom_call_target="tpu_custom_call" | custom-call | flops 78643200 | bytes 6291456 | tf_op jit(solution)/shard_map/pallas_call | solution.py:857
  61.3 3.9 %shard_map.139 = (f32[32,2,8,1024]{3,2,1,0:T(8,128)}, f32[2,8,256]{2,1,0:T(8,128)}, f32[2,8,256]{2,1,0:T(8,128)}, f32[2,8,256]{2,1,0:T(8,128)}) custom-call(s32[32]{0:T(128)} %age.3, f32[32]{0:T(128)} %mass.3, f32[32,2,8,1024]{3,2,1,0:T(8,128)} %get-tuple-element.7.last, f32[2,8,1024]{2,1,0:T(8,128)} %get-tuple-element.8.press, ...), custom_call_target="tpu_custom_call" | custom-call | flops 1048576 | bytes 4194304 | tf_op jit(solution)/shard_map/pallas_call | solution.py:874

commit v5 on v3

--- a/solution.py
+++ b/solution.py
@@ -104,7 +104,7 @@
 
     get_dens = fetch(dens_in, dens, 0)
     get_cot = fetch(cot_in, cot, 1)
-    for copy in get_dens + get_cot:
+    for copy in get_cot + get_dens:
         copy.start()
     every = cohorts * n_coh
     lat = lax.axis_index("lat")
@@ -262,6 +262,14 @@
     )
     for layer in range(layers):
         send(FIELDS, layer)
+    for copy in get_cot:
+        copy.wait()
+    for layer in range(layers):
+        pack(cot, layer, 0, rows - 1, cot1_o)
+        send(COT1, layer)
+    for layer in range(layers):
+        pack(cot, layer, 1, rows - 2, cot2_o)
+        send(COT2, layer)
     for copy in get_dens:
         copy.wait()
 
@@ -299,14 +307,6 @@
         one = age[cohort]
         for index, table in enumerate((mort, crowd_coef, mass, speed)):
             params[index, cohort : cohort + 1, :] = jnp.full((1, 128), table[one], jnp.float32)
-    for copy in get_cot:
-        copy.wait()
-    for layer in range(layers):
-        pack(cot, layer, 0, rows - 1, cot1_o)
-        send(COT1, layer)
-    for layer in range(layers):
-        pack(cot, layer, 1, rows - 2, cot2_o)
-        send(COT2, layer)
     for layer in range(layers):
         pack(dens, layer, 0, rows - 1, dens_edge)
     grads[...] = jnp.zeros(grads.shape, jnp.float32)

time: 62.4 us -> 62.4 us (level)
  no operation moved by 1% of the time
where the time goes in v5:
time: 62.4 us; the launch traced here: 62.2 us
  Pallas kernels  61.5 us (99%)
  between operations  0.64 us (1%)
    pallas_call x1, Pallas kernels, local(): pl.pallas_call(functools.partial(kernel, n_lat, n_coh), out_shape=(jax.Sh...  57.6 us
    pallas_call x1, Pallas kernels, local(): pl.pallas_call(finish, out_shape=(jax.ShapeDtypeStruct(density.shape, f32...  3.9 us

profile of v5, /device:TPU:0, one launch (start us, length us, event | category | flops | bytes accessed | tf_op | source)
XLA Modules:
  0.0 62.2 jit_solution(13244398089980554810)
XLA Ops:
  0.6 57.6 %shard_map.138 = (f32[32,2,8,1024]{3,2,1,0:T(8,128)}, f32[2,8,1024]{2,1,0:T(8,128)}, f32[3,2,8,256]{3,2,1,0:T(8,128)}) custom-call(f32[32,2,8,1024]{3,2,1,0:T(8,128)} %dens_in.1, f32[32,2,8,1024]{3,2,1,0:T(8,128)} %cot_in.1, s32[2,8,1024]{2,1,0:T(8,128)} %land.1, f32[2,8,1024]{2,1,0:T(8,128)} %east.1, f32[2,8,1024]{2,1,0:T(8,128)} %north.1, ...), custom_call_target="tpu_custom_call" | custom-call | flops 78643200 | bytes 6291456 | tf_op jit(solution)/shard_map/pallas_call | solution.py:760
  58.3 3.9 %shard_map.139 = (f32[32,2,8,1024]{3,2,1,0:T(8,128)}, f32[2,8,256]{2,1,0:T(8,128)}, f32[2,8,256]{2,1,0:T(8,128)}, f32[2,8,256]{2,1,0:T(8,128)}) custom-call(s32[32]{0:T(128)} %age.3, f32[32]{0:T(128)} %mass.3, f32[32,2,8,1024]{3,2,1,0:T(8,128)} %get-tuple-element.7.last, f32[2,8,1024]{2,1,0:T(8,128)} %get-tuple-element.8.press, ...), custom_call_target="tpu_custom_call" | custom-call | flops 1048576 | bytes 4194304 | tf_op jit(solution)/shard_map/pallas_call | solution.py:777
